TPU v7x, 128 devices: a whole 4x4x4 slice. The times are simulated.
128 devices in a mesh: row: 8 (over y, core), col: 16 (over x, z).
Axes of the slice: x: 4, y: 4, z: 4, core: 2. Of those that a mesh axis runs over, the one named last changes fastest.
Arguments:
- alias_factors: bfloat16 [16384, 256], P(('row', 'col')), may hold values from -1.5 to 1.5
- entity_factors: bfloat16 [32768, 256], P(('row', 'col')), may hold values from -1.5 to 1.5
- tile_ids: int32 [8, 16, 96, 2], P('row', 'col'), may hold values from 0 to 15, as said below
- tile_score: bfloat16 [8, 16, 96, 128, 128], P('row', 'col'), may hold values from -6 to 6
- tile_weight: bfloat16 [8, 16, 96, 128, 128], P('row', 'col'), may hold values from 0 to 4, as said below
Outputs:
- alias_new: bfloat16 [16384, 256], P(('row', 'col'))
- entity_new: bfloat16 [32768, 256], P(('row', 'col'))
Inputs may be any that keep to these rules, and one draw needn't show every extreme that they name: `tile_ids`: column 0 names a local alias block 0 to 15 of the device's row group, column 1 a local entity block 0 to 15 of its column group; the first min(96, 16) tiles name alias blocks 0, 1, 2 and on in order, the first min(96, 16) tiles name entity blocks likewise; pairs may repeat. `tile_weight`: about half of the entries are observed and positive, the rest zero.
All inputs are finite; a program needn't handle non-finite values.
Results may differ from a plain program's by a relative error of at most 0.012.
The roundings to bfloat16 on the way count: a program that leaves them out, or rounds other values in their place, can miss the bound.
Values may be sent and summed in bfloat16 or wider, within the bound.
A program may use at most 128 MiB of HBM per device.

v0:
```python
import jax
import jax.numpy as jnp
from jax import lax
from jax.sharding import PartitionSpec as P

ridge = 1.0
eps = 1e-06


def tile_terms(alias_t, entity_t, score, weight, own_alias, residual):
    product = jnp.einsum("tak,tek->tae", alias_t, entity_t, preferred_element_type=jnp.float32)
    if residual:
        error = weight.astype(jnp.float32) * (score.astype(jnp.float32) - product)
    else:
        error = weight.astype(jnp.float32) * product
    error = error.astype(jnp.bfloat16)
    if own_alias:
        return jnp.einsum("tae,tek->tak", error, entity_t, preferred_element_type=jnp.float32)
    return jnp.einsum("tae,tak->tek", error, alias_t, preferred_element_type=jnp.float32)


def collect(terms, target, count):
    onehot = (target[None, :] == jnp.arange(count, dtype=jnp.int32)[:, None]).astype(jnp.float32)
    summed = jnp.einsum("at,tpk->apk", onehot, terms, precision=lax.Precision.HIGHEST)
    return summed.reshape(count * terms.shape[1], terms.shape[2])


def cg_update(x_rows, resid, direction, image, norm_now):
    curve = jnp.sum(direction * image, axis=-1, keepdims=True)
    alpha = norm_now / (curve + eps)
    x_rows = x_rows + alpha * direction
    resid = resid - alpha * image
    norm_next = jnp.sum(resid * resid, axis=-1, keepdims=True)
    direction = resid + norm_next / (norm_now + eps) * direction
    return (x_rows, resid, direction, norm_next)


def on_device(alias_factors, entity_factors, tile_ids, tile_score, tile_weight):
    block = tile_score.shape[-1]
    rank = alias_factors.shape[1]
    own_alias_rows = alias_factors.shape[0]
    n_alias = lax.axis_size("col") * (own_alias_rows // block)
    n_entity = lax.axis_size("row") * (entity_factors.shape[0] // block)
    pairs = tile_ids[0, 0]
    alias_ids = pairs[:, 0]
    entity_ids = pairs[:, 1]
    score = tile_score[0, 0]
    weight = tile_weight[0, 0]
    entity_group = lax.all_gather(entity_factors, "row", axis=0, tiled=True).reshape(
        n_entity, block, rank
    )
    alias_group = lax.all_gather(alias_factors, "col", axis=0, tiled=True).reshape(
        n_alias, block, rank
    )
    entity_tiles = jnp.take(entity_group, entity_ids, axis=0)

    def alias_terms(alias_vec, residual):
        alias_t = jnp.take(alias_vec, alias_ids, axis=0)
        terms = tile_terms(alias_t, entity_tiles, score, weight, True, residual)
        return collect(terms, alias_ids, n_alias)

    def alias_share(partial_value):
        return lax.psum_scatter(partial_value, "col", scatter_dimension=0, tiled=True)

    x_rows = alias_factors.astype(jnp.float32)
    resid = alias_share(alias_terms(alias_group, True)) - ridge * x_rows
    direction = resid
    norm_now = jnp.sum(resid * resid, axis=-1, keepdims=True)
    for step_index in range(2):
        direction_bf = direction.astype(jnp.bfloat16)
        spread = lax.all_gather(direction_bf, "col", axis=0, tiled=True).reshape(
            n_alias, block, rank
        )
        image = alias_share(alias_terms(spread, False)) + ridge * direction
        x_rows, resid, direction, norm_now = cg_update(x_rows, resid, direction, image, norm_now)
    alias_new = x_rows.astype(jnp.bfloat16)
    alias_full = lax.all_gather(alias_new, "col", axis=0, tiled=True).reshape(n_alias, block, rank)
    alias_tiles = jnp.take(alias_full, alias_ids, axis=0)

    def entity_share(entity_vec, residual):
        entity_t = jnp.take(entity_vec, entity_ids, axis=0)
        terms = tile_terms(alias_tiles, entity_t, score, weight, False, residual)
        return lax.psum_scatter(
            collect(terms, entity_ids, n_entity), "row", scatter_dimension=0, tiled=True
        )

    x_rows = entity_factors.astype(jnp.float32)
    resid = entity_share(entity_group, True) - ridge * x_rows
    direction = resid
    norm_now = jnp.sum(resid * resid, axis=-1, keepdims=True)
    for step_index in range(2):
        direction_bf = direction.astype(jnp.bfloat16)
        spread = lax.all_gather(direction_bf, "row", axis=0, tiled=True).reshape(
            n_entity, block, rank
        )
        image = entity_share(spread, False) + ridge * direction
        x_rows, resid, direction, norm_now = cg_update(x_rows, resid, direction, image, norm_now)
    entity_new = x_rows.astype(jnp.bfloat16)
    return (alias_new, entity_new)


def solution(mesh):
    placed = (
        P(("row", "col"), None),
        P(("row", "col"), None),
        P("row", "col", None, None),
        P("row", "col", None, None, None),
        P("row", "col", None, None, None),
    )
    return jax.shard_map(
        on_device,
        mesh=mesh,
        in_specs=placed,
        out_specs=(P(("row", "col"), None), P(("row", "col"), None)),
        check_vma=False,
    )
```

profile of v0, /device:TPU:0, one launch (start us, length us, event | category | flops | bytes accessed | tf_op | source)
XLA Modules:
  0.0 827.3 jit_solution(9531479513046375090)
XLA Ops:
  8.7 0.8 compare_and_fusion
  10.2 25.4 %all-gather.10.cloned.1.call-done = bf16[2048,256]{1,0:T(8,128)(2,1)} async-done(((bf16[256,256]{1,0:T(8,128)(2,1)}), bf16[2048,256]{1,0:T(8,128)(2,1)}) %all-gather.10.cloned.1.call-update) | async-done | bytes 1048592 | tf_op jit(solution)/shard_map/all_gather | solution.py:49
  35.6 7.2 gather_fusion.1
  42.8 37.7 %all-gather.8.cloned.1.call-done = bf16[2048,256]{1,0:T(8,128)(2,1)} async-done(((bf16[128,256]{1,0:T(8,128)(2,1)}), bf16[2048,256]{1,0:T(8,128)(2,1)}) %all-gather.8.cloned.1.call-update) | async-done | bytes 1048592 | tf_op jit(solution)/shard_map/all_gather | solution.py:52
  80.5 7.2 gather_fusion
  87.6 14.8 %fusion.43 = f32[96,128,256]{2,1,0:T(8,128)} fusion(bf16[1,1,96,128,128]{4,3,2,1,0:T(8,128)(2,1)} %param.10, bf16[1,1,96,128,128]{4,3,2,1,0:T(8,128)(2,1)} %param.11, bf16[96,128,256]{2,1,0:T(8,128)(2,1)} %gather_fusion, pred[96]{0:T(512)(128)(4,1)S(1)} %get-tuple-element.19, bf16[96,128,256]{2,1,0:T(8,128)(2,1)} %gather_fusion.1, ...), kind=kOutput, calls=%fused_computation.55 | convolution fusion | flops 1627914240 | bytes 31457472 | tf_op jit(solution)/shard_map/tae,tek->tak/dot_general | solution.py:18
  102.4 15.6 %fusion.10 = f32[16,128,256]{2,0,1:T(8,128)S(1)} fusion(f32[96,128,256]{2,1,0:T(8,128)} %fusion.43, s32[96]{0:T(128)S(1)} %get-tuple-element.18), kind=kOutput, calls=%fused_computation.23 | convolution fusion | flops 603981312 | bytes 14680448 | tf_op jit(solution)/shard_map/at,tpk->apk/dot_general | solution.py:24
  118.1 2.6 copy.7
  120.8 73.9 %reduce-scatter.7.cloned.1.call-done = f32[128,256]{1,0:T(8,128)} async-done(((f32[2048,256]{1,0:T(8,128)}), f32[128,256]{1,0:T(8,128)}) %reduce-scatter.7.cloned.1.call-update) | async-done | bytes 131088 | tf_op jit(solution)/shard_map/reduce_scatter | solution.py:63
  194.6 1.5 fusion.113
  196.2 43.2 %all-gather.12.cloned.1.call-done = bf16[2048,256]{1,0:T(8,128)(2,1)} async-done(((bf16[128,256]{1,0:T(8,128)(2,1)}), bf16[2048,256]{1,0:T(8,128)(2,1)}) %all-gather.12.cloned.1.call-update) | async-done | bytes 1048592 | tf_op jit(solution)/shard_map/all_gather | solution.py:71
  239.4 7.2 gather_fusion.2
  246.6 12.9 %fusion.41 = f32[96,128,256]{2,1,0:T(8,128)} fusion(bf16[1,1,96,128,128]{4,3,2,1,0:T(8,128)(2,1)} %param.11, bf16[96,128,256]{2,1,0:T(8,128)(2,1)} %gather_fusion.2, pred[96]{0:T(512)(128)(4,1)S(1)} %get-tuple-element.19, bf16[96,128,256]{2,1,0:T(8,128)(2,1)} %gather_fusion.1, pred[96]{0:T(512)(128)(4,1)S(1)} %get-tuple-element.13), kind=kOutput, calls=%fused_computation.54 | convolution fusion | flops 1624768512 | bytes 28311744 | tf_op jit(solution)/shard_map/tae,tek->tak/dot_general | solution.py:18
  259.5 15.3 %fusion.8 = f32[16,128,256]{2,0,1:T(8,128)S(1)} fusion(f32[96,128,256]{2,1,0:T(8,128)} %fusion.41, s32[96]{0:T(128)S(1)} %get-tuple-element.18), kind=kOutput, calls=%fused_computation.21 | convolution fusion | flops 603981312 | bytes 14680448 | tf_op jit(solution)/shard_map/at,tpk->apk/dot_general | solution.py:24
  274.8 2.6 copy.8
  277.5 73.8 %reduce-scatter.9.cloned.1.call-done = f32[128,256]{1,0:T(8,128)} async-done(((f32[2048,256]{1,0:T(8,128)}), f32[128,256]{1,0:T(8,128)}) %reduce-scatter.9.cloned.1.call-update) | async-done | bytes 131088 | tf_op jit(solution)/shard_map/reduce_scatter | solution.py:63
  351.3 1.0 multiply_reduce_fusion.4
  353.3 42.6 %all-gather.14.cloned.1.call-done = bf16[2048,256]{1,0:T(8,128)(2,1)} async-done(((bf16[128,256]{1,0:T(8,128)(2,1)}), bf16[2048,256]{1,0:T(8,128)(2,1)}) %all-gather.14.cloned.1.call-update) | async-done | bytes 1048592 | tf_op jit(solution)/shard_map/all_gather | solution.py:71
  395.9 7.3 gather_fusion.3
  403.2 12.9 %fusion.39 = f32[96,128,256]{2,1,0:T(8,128)} fusion(bf16[1,1,96,128,128]{4,3,2,1,0:T(8,128)(2,1)} %param.11, bf16[96,128,256]{2,1,0:T(8,128)(2,1)} %gather_fusion.3, pred[96]{0:T(512)(128)(4,1)S(1)} %get-tuple-element.19, bf16[96,128,256]{2,1,0:T(8,128)(2,1)} %gather_fusion.1, pred[96]{0:T(512)(128)(4,1)S(1)} %get-tuple-element.13), kind=kOutput, calls=%fused_computation.53 | convolution fusion | flops 1624768512 | bytes 28311744 | tf_op jit(solution)/shard_map/tae,tek->tak/dot_general | solution.py:18
  416.1 15.3 %fusion.6 = f32[16,128,256]{2,0,1:T(8,128)S(1)} fusion(f32[96,128,256]{2,1,0:T(8,128)} %fusion.39, s32[96]{0:T(128)S(1)} %get-tuple-element.18), kind=kOutput, calls=%fused_computation.19 | convolution fusion | flops 603981312 | bytes 14680448 | tf_op jit(solution)/shard_map/at,tpk->apk/dot_general | solution.py:24
  431.4 2.6 copy.9
  434.1 73.9 %reduce-scatter.11.cloned.1.call-done = f32[128,256]{1,0:T(8,128)} async-done(((f32[2048,256]{1,0:T(8,128)}), f32[128,256]{1,0:T(8,128)}) %reduce-scatter.11.cloned.1.call-update) | async-done | bytes 131088 | tf_op jit(solution)/shard_map/reduce_scatter | solution.py:63
  507.9 1.1 fusion.85
  509.0 0.8 fusion.84
  509.9 43.1 %all-gather.16.cloned.1.call-done = bf16[2048,256]{1,0:T(8,128)(2,1)} async-done(((bf16[128,256]{1,0:T(8,128)(2,1)}), bf16[2048,256]{1,0:T(8,128)(2,1)}) %all-gather.16.cloned.1.call-update) | async-done | bytes 1048592 | tf_op jit(solution)/shard_map/all_gather | solution.py:77
  552.9 7.4 gather_fusion.4
  560.3 14.8 %fusion.37 = f32[96,128,256]{2,1,0:T(8,128)} fusion(bf16[1,1,96,128,128]{4,3,2,1,0:T(8,128)(2,1)} %param.10, bf16[1,1,96,128,128]{4,3,2,1,0:T(8,128)(2,1)} %param.11, bf16[96,128,256]{2,1,0:T(8,128)(2,1)} %gather_fusion.4, pred[96]{0:T(512)(128)(4,1)S(1)} %get-tuple-element.19, bf16[96,128,256]{2,1,0:T(8,128)(2,1)} %gather_fusion.1, ...), kind=kOutput, calls=%fused_computation.52 | convolution fusion | flops 1627914240 | bytes 31457472 | tf_op jit(solution)/shard_map/tae,tak->tek/dot_general | solution.py:19
  575.1 15.3 %fusion.4 = f32[16,128,256]{2,0,1:T(8,128)S(1)} fusion(f32[96,128,256]{2,1,0:T(8,128)} %fusion.37, s32[96]{0:T(128)S(1)} %get-tuple-element.17), kind=kOutput, calls=%fused_computation.17 | convolution fusion | flops 603981312 | bytes 14680448 | tf_op jit(solution)/shard_map/at,tpk->apk/dot_general | solution.py:24
  590.4 2.6 copy.10
  593.1 33.0 %reduce-scatter.13.cloned.1.call-done = f32[256,256]{1,0:T(8,128)} async-done(((f32[2048,256]{1,0:T(8,128)}), f32[256,256]{1,0:T(8,128)}) %reduce-scatter.13.cloned.1.call-update) | async-done | bytes 262160 | tf_op jit(solution)/shard_map/reduce_scatter | solution.py:83
  626.1 1.6 fusion.112
  627.8 22.8 %all-gather.18.cloned.1.call-done = bf16[2048,256]{1,0:T(8,128)(2,1)} async-done(((bf16[256,256]{1,0:T(8,128)(2,1)}), bf16[2048,256]{1,0:T(8,128)(2,1)}) %all-gather.18.cloned.1.call-update) | async-done | bytes 1048592 | tf_op jit(solution)/shard_map/all_gather | solution.py:93
  650.6 7.6 gather_fusion.5
  658.2 12.8 %fusion.35 = f32[96,128,256]{2,1,0:T(8,128)} fusion(bf16[1,1,96,128,128]{4,3,2,1,0:T(8,128)(2,1)} %param.11, bf16[96,128,256]{2,1,0:T(8,128)(2,1)} %gather_fusion.5, pred[96]{0:T(512)(128)(4,1)S(1)} %get-tuple-element.13, bf16[96,128,256]{2,1,0:T(8,128)(2,1)} %gather_fusion.4, pred[96]{0:T(512)(128)(4,1)S(1)} %get-tuple-element.19), kind=kOutput, calls=%fused_computation.51 | convolution fusion | flops 1624768512 | bytes 28311744 | tf_op jit(solution)/shard_map/tae,tak->tek/dot_general | solution.py:19
  670.9 15.3 %fusion.2 = f32[16,128,256]{2,0,1:T(8,128)S(1)} fusion(f32[96,128,256]{2,1,0:T(8,128)} %fusion.35, s32[96]{0:T(128)S(1)} %get-tuple-element.17), kind=kOutput, calls=%fused_computation.15 | convolution fusion | flops 603981312 | bytes 14680448 | tf_op jit(solution)/shard_map/at,tpk->apk/dot_general | solution.py:24
  686.2 2.6 copy.11
  688.9 33.6 %reduce-scatter.15.cloned.1.call-done = f32[256,256]{1,0:T(8,128)} async-done(((f32[2048,256]{1,0:T(8,128)}), f32[256,256]{1,0:T(8,128)}) %reduce-scatter.15.cloned.1.call-update) | async-done | bytes 262160 | tf_op jit(solution)/shard_map/reduce_scatter | solution.py:83
  722.5 1.1 multiply_reduce_fusion.1
  723.8 0.8 fusion.111
  724.7 22.3 %all-gather.20.cloned.1.call-done = bf16[2048,256]{1,0:T(8,128)(2,1)} async-done(((bf16[256,256]{1,0:T(8,128)(2,1)}), bf16[2048,256]{1,0:T(8,128)(2,1)}) %all-gather.20.cloned.1.call-update) | async-done | bytes 1048592 | tf_op jit(solution)/shard_map/all_gather | solution.py:93
  747.0 7.3 gather_fusion.6
  754.3 12.8 %fusion.33 = f32[96,128,256]{2,1,0:T(8,128)} fusion(bf16[1,1,96,128,128]{4,3,2,1,0:T(8,128)(2,1)} %param.11, bf16[96,128,256]{2,1,0:T(8,128)(2,1)} %gather_fusion.6, pred[96]{0:T(512)(128)(4,1)S(1)} %get-tuple-element.13, bf16[96,128,256]{2,1,0:T(8,128)(2,1)} %gather_fusion.4, pred[96]{0:T(512)(128)(4,1)S(1)} %get-tuple-element.19), kind=kOutput, calls=%fused_computation.50 | convolution fusion | flops 1624768512 | bytes 28311744 | tf_op jit(solution)/shard_map/tae,tak->tek/dot_general | solution.py:19
  767.1 15.3 %fusion = f32[16,128,256]{2,0,1:T(8,128)S(1)} fusion(f32[96,128,256]{2,1,0:T(8,128)} %fusion.33, s32[96]{0:T(128)S(1)} %get-tuple-element.17), kind=kOutput, calls=%fused_computation.13 | convolution fusion | flops 603981312 | bytes 14680448 | tf_op jit(solution)/shard_map/at,tpk->apk/dot_general | solution.py:24
  782.4 2.6 copy.12
  785.0 33.6 %reduce-scatter.17.cloned.1.call-done = f32[256,256]{1,0:T(8,128)} async-done(((f32[2048,256]{1,0:T(8,128)}), f32[256,256]{1,0:T(8,128)}) %reduce-scatter.17.cloned.1.call-update) | async-done | bytes 262160 | tf_op jit(solution)/shard_map/reduce_scatter | solution.py:83
  818.6 1.2 fusion.82
  819.7 0.8 fusion.81
  (41 shorter events, 4.0 us)
Async XLA Ops:
  7.2 28.4 %all-gather.10.cloned.1.call-start = ((), (), s32[]{:S(2)}) async-start(), calls=%async_computation.7 | async-start | bytes 1179648 | tf_op jit(solution)/shard_map/all_gather | solution.py:49
  7.9 72.6 %all-gather.8.cloned.1.call-start = ((), (), s32[]{:S(2)}) async-start(), calls=%async_computation.6 | async-start | bytes 1114112 | tf_op jit(solution)/shard_map/all_gather | solution.py:52
  8.6 186.0 %reduce-scatter.7.cloned.1.call-start = ((), (), s32[]{:S(2)}) async-start(), calls=%async_computation.8 | async-start | bytes 2228224 | tf_op jit(solution)/shard_map/reduce_scatter | solution.py:63
  118.1 76.5 %copy-start.1 = (bf16[128,256]{1,0:T(8,128)(2,1)S(1)}, bf16[128,256]{1,0:T(8,128)(2,1)}, u32[]{:S(2)}) copy-start(bf16[128,256]{1,0:T(8,128)(2,1)} %param.7) | copy-start | bytes 196612
  120.7 118.7 %all-gather.12.cloned.1.call-start = ((), (), s32[]{:S(2)}) async-start(), calls=%async_computation.9 | async-start | bytes 1114112 | tf_op jit(solution)/shard_map/all_gather | solution.py:71
  196.2 155.1 %reduce-scatter.9.cloned.1.call-start = ((), (), s32[]{:S(2)}) async-start(), calls=%async_computation.10 | async-start | bytes 2228224 | tf_op jit(solution)/shard_map/reduce_scatter | solution.py:63
  277.4 118.5 %all-gather.14.cloned.1.call-start = ((), (), s32[]{:S(2)}) async-start(), calls=%async_computation.11 | async-start | bytes 1114112 | tf_op jit(solution)/shard_map/all_gather | solution.py:71
  353.3 154.7 %reduce-scatter.11.cloned.1.call-start = ((), (), s32[]{:S(2)}) async-start(), calls=%async_computation.12 | async-start | bytes 2228224 | tf_op jit(solution)/shard_map/reduce_scatter | solution.py:63
  434.0 118.9 %all-gather.16.cloned.1.call-start = ((), (), s32[]{:S(2)}) async-start(), calls=%async_computation.13 | async-start | bytes 1114112 | tf_op jit(solution)/shard_map/all_gather | solution.py:77
  509.8 116.2 %reduce-scatter.13.cloned.1.call-start = ((), (), s32[]{:S(2)}) async-start(), calls=%async_computation.14 | async-start | bytes 2359296 | tf_op jit(solution)/shard_map/reduce_scatter | solution.py:83
  590.4 35.6 %copy-start = (bf16[256,256]{1,0:T(8,128)(2,1)S(1)}, bf16[256,256]{1,0:T(8,128)(2,1)}, u32[]{:S(2)}) copy-start(bf16[256,256]{1,0:T(8,128)(2,1)} %param.8) | copy-start | bytes 393220
  593.0 57.6 %all-gather.18.cloned.1.call-start = ((), (), s32[]{:S(2)}) async-start(), calls=%async_computation.15 | async-start | bytes 1179648 | tf_op jit(solution)/shard_map/all_gather | solution.py:93
  627.7 94.7 %reduce-scatter.15.cloned.1.call-start = ((), (), s32[]{:S(2)}) async-start(), calls=%async_computation.16 | async-start | bytes 2359296 | tf_op jit(solution)/shard_map/reduce_scatter | solution.py:83
  688.8 58.1 %all-gather.20.cloned.1.call-start = ((), (), s32[]{:S(2)}) async-start(), calls=%async_computation.17 | async-start | bytes 1179648 | tf_op jit(solution)/shard_map/all_gather | solution.py:93
  724.6 93.9 %reduce-scatter.17.cloned.1.call-start = ((), (), s32[]{:S(2)}) async-start(), calls=%async_computation.18 | async-start | bytes 2359296 | tf_op jit(solution)/shard_map/reduce_scatter | solution.py:83
Sparse Core Ops, SparseCore 0:
  9.7 25.8 all-gather.9
  37.7 42.6 all-gather.7
  120.8 73.7 reduce-scatter.6
  197.4 41.9 all-gather.11
  277.5 73.6 reduce-scatter.8
  353.8 41.9 all-gather.13
  434.1 73.7 reduce-scatter.10
  510.9 42.0 all-gather.15
  593.2 32.8 reduce-scatter.12
  628.3 22.2 all-gather.17
  689.0 33.4 reduce-scatter.14
  724.7 22.1 all-gather.19
  785.1 33.4 reduce-scatter.16
where the time goes:
time: 841 us; the launch traced here: 827 us
  waiting for transfers between devices  560 us (67%)
  matrix products  173 us (21%)
  local copies, waits for them, and re-layouts  67.3 us (8%)
  between operations  14.2 us (2%)
  other arithmetic  11.9 us (1%)
    reduce_scatter x3, waiting for transfers between devices, alias_share(): lax.psum_scatter(partial_value, 'col', scatter_dimension=0, tiled=True)  222 us
    reduce_scatter x3, waiting for transfers between devices, entity_share(): lax.psum_scatter(collect(terms, entity_ids, n_entity), 'row', scatter_dim...  100 us
    dot_general x6, matrix products, collect(): jnp.einsum('at,tpk->apk', onehot, terms, precision=lax.Precision.HIGHEST)  92.2 us
    all_gather x2, waiting for transfers between devices, on_device(): lax.all_gather(direction_bf, 'col', axis=0, tiled=True)  85.8 us
    all_gather x2, waiting for transfers between devices, on_device(): lax.all_gather(direction_bf, 'row', axis=0, tiled=True)  45.1 us
    all_gather x1, waiting for transfers between devices, on_device(): lax.all_gather(alias_new, 'col', axis=0, tiled=True)  43.1 us
    dot_general x3, matrix products, tile_terms(): jnp.einsum('tae,tek->tak', error, entity_t, preferred_element_type=jnp.fl...  40.7 us
    dot_general x3, matrix products, tile_terms(): jnp.einsum('tae,tak->tek', error, alias_t, preferred_element_type=jnp.flo...  40.3 us
  transfers between devices with their start and end apart: 13, of which 13 were waited for; matrix products, arithmetic and copies ran while one was open for 1% of the time, Pallas kernels for 0%

commit v1 on v0

v1 whole, which is shorter than its diff:
```python
import functools

import jax
import jax.numpy as jnp
from jax import lax
from jax.experimental import pallas as pl
from jax.experimental.pallas import tpu as pltpu
from jax.sharding import PartitionSpec as P

ridge = 1.0
eps = 1e-06
MESH = pl.DeviceIdType.MESH
F32 = jnp.float32
BF16 = jnp.bfloat16
B = 128
K = 256
T = 96
NB = 16
PAIRS = (T + NB) // 2
STEP = 4

A_TILE, A_OTHER, A_KEY, A_SWAP, A_KEEP, A_LAST = range(6)
E_TILE, E_OTHER, E_KEY, E_KEEP, E_LAST = range(6, 11)


def plan_kernel(ids_ref, out_ref):
    ids = ids_ref[...].astype(F32)
    row_i = lax.broadcasted_iota(jnp.int32, (T, 128), 0).astype(F32)
    lane_i = lax.broadcasted_iota(jnp.int32, (T, 128), 1).astype(F32)
    out_ref[...] = jnp.zeros_like(out_ref)

    def put(row, value):
        out_ref[row : row + 1, :] = value.astype(jnp.int32)

    for key, other, rows in (
        (0, 1, (A_TILE, A_OTHER, A_KEY, A_KEEP, A_LAST)),
        (1, 0, (E_TILE, E_OTHER, E_KEY, E_KEEP, E_LAST)),
    ):
        kc = jnp.broadcast_to(ids[:, key : key + 1], (T, 128))
        oc = jnp.broadcast_to(ids[:, other : other + 1], (T, 128))
        kr = jnp.sum(jnp.where(row_i == lane_i, kc + 1.0, 0.0), axis=0, keepdims=True) - 1.0
        same = jnp.where(kc == kr, 1.0, 0.0)
        rank = jnp.sum(jnp.where(lane_i < row_i, same, 0.0), axis=1, keepdims=True)
        count = jnp.sum(same, axis=1, keepdims=True)
        odd = count - 2.0 * jnp.floor(count * 0.5)
        width = 1.0 + jnp.where(rank == 0.0, odd, 0.0)
        width = jnp.broadcast_to(width, (T, 128))
        n_row = jnp.sum(jnp.where(kc == lane_i, width, 0.0), axis=0, keepdims=True)
        start = jnp.sum(
            jnp.where(lane_i < kc, jnp.broadcast_to(n_row, (T, 128)), 0.0), axis=1, keepdims=True
        )
        pos = jnp.broadcast_to(start + rank, (T, 128))
        hit = jnp.where(pos == lane_i, 1.0, 0.0)
        valid = jnp.sum(hit, axis=0, keepdims=True)
        put(rows[0], jnp.sum(hit * row_i, axis=0, keepdims=True) + T * (1.0 - valid))
        put(rows[1], jnp.sum(hit * oc, axis=0, keepdims=True))
        key_row = jnp.sum(hit * kc, axis=0, keepdims=True)
        put(rows[2], key_row)
        if key == 0:
            high = jnp.floor(key_row * 0.25)
            put(A_SWAP, (key_row - 4.0 * high) * 4.0 + high)
        keep = jnp.where(jnp.broadcast_to(rank, (T, 128)) > 0.0, hit, 0.0)
        put(rows[3], jnp.sum(keep, axis=0, keepdims=True))
        upto = jnp.sum(jnp.where(kc <= lane_i, width, 0.0), axis=0, keepdims=True)
        put(rows[4], upto * 0.5 - 1.0)


class Copies:
    def __init__(self, send, recv):
        self.send, self.recv, self.all = send, recv, []

    def start(self, src, dst, device):
        n = len(self.all)
        cp = pltpu.make_async_remote_copy(
            src_ref=src,
            dst_ref=dst,
            send_sem=self.send.at[n],
            recv_sem=self.recv.at[n],
            device_id=device,
            device_id_type=MESH,
        )
        cp.start()
        self.all.append(cp)
        return cp


N_COPIES = 12 * 4 + 12 * 2 + 7 * 3 + 7 * 2 + 15 + 7


def sweep_kernel(
    plan, x_in, y_in, w_hbm, s_hbm, x_out, y_out,
    w, s, wt, st, xn, run, run_c,
    ga, gb, gy, sa, sb, ra, rb, ta, tb, qa, qb,
    se, me, te, qe, cmsg, emsg, vx, vr, vd, ux, ur, ud,
    send, recv, lsem,
):
    row = lax.axis_index("row")
    col = lax.axis_index("col")
    cy, cc = row // 2, row % 2
    cx, cz = col // 4, col % 4

    def at_x(d):
        return (row, lax.rem(cx + d, 4) * 4 + cz)

    def at_z(d):
        return (row, cx * 4 + lax.rem(cz + d, 4))

    def at_y(d):
        return (lax.rem(cy + d, 4) * 2 + cc, col)

    mate = (cy * 2 + (1 - cc), col)

    copies = Copies(send, recv)
    load_w = pltpu.make_async_copy(w_hbm.at[0, 0], w.at[pl.ds(0, T)], lsem.at[0])
    load_s = pltpu.make_async_copy(s_hbm.at[0, 0], s.at[pl.ds(0, T)], lsem.at[1])
    load_w.start()
    load_s.start()

    barrier = pltpu.get_barrier_semaphore()
    for d in range(1, 16):
        pl.semaphore_signal(barrier, 1, device_id=(row, lax.rem(col + d, 16)), device_id_type=MESH)
    for d in range(1, 8):
        pl.semaphore_signal(barrier, 1, device_id=(lax.rem(row + d, 8), col), device_id_type=MESH)
    pl.semaphore_wait(barrier, 22)

    eye = jnp.where(
        lax.broadcasted_iota(jnp.int32, (B, B), 0) == lax.broadcasted_iota(jnp.int32, (B, B), 1),
        1.0, 0.0,
    ).astype(F32)

    def to_row(column):
        return jnp.sum(jnp.broadcast_to(column, (B, B)) * eye, axis=0, keepdims=True)

    def to_column(line):
        return jnp.sum(jnp.broadcast_to(line, (B, B)) * eye, axis=1, keepdims=True)

    slot_a = cz * 4 + cx
    slot_b = cx * 4 + cz

    def alias_gather(i, value):
        ga[i][slot_a] = value[:, :B]
        gb[i][slot_b] = value[:, B:]
        first_a = [copies.start(ga[i].at[slot_a], ga[i].at[slot_a], at_x(d)) for d in (1, 3, 2)]
        first_b = [copies.start(gb[i].at[slot_b], gb[i].at[slot_b], at_z(d)) for d in (1, 3, 2)]

        def middle():
            for cp in first_a:
                cp.wait_recv()
            rows_a = pl.ds(cz * 4, 4)
            second = [copies.start(ga[i].at[rows_a], ga[i].at[rows_a], at_z(d)) for d in (1, 3, 2)]
            for cp in first_b:
                cp.wait_recv()
            rows_b = pl.ds(cx * 4, 4)
            second += [copies.start(gb[i].at[rows_b], gb[i].at[rows_b], at_x(d)) for d in (1, 3, 2)]
            return second

        return middle

    def finish(second):
        for cp in second:
            cp.wait_recv()

    def alias_spread(i):
        for b in range(NB):
            block = run[plan[A_LAST, b] + 1]
            sa[i, (b % 4) * 4 + b // 4] = block[:, :B].astype(BF16)
            sb[i, b] = block[:, B:].astype(BF16)
        first_a, first_b = [], []
        for n, d in enumerate((1, 3, 2)):
            rows_a = pl.ds(lax.rem(cz + d, 4) * 4, 4)
            first_a.append(copies.start(sa.at[i, rows_a], ra.at[i, n], at_z(d)))
            rows_b = pl.ds(lax.rem(cx + d, 4) * 4, 4)
            first_b.append(copies.start(sb.at[i, rows_b], rb.at[i, n], at_x(d)))

        def middle():
            second = []
            for first, sx, rx, tx, qx, base, own, at in (
                (first_a, sa, ra, ta, qa, cz * 4, cx, at_x),
                (first_b, sb, rb, tb, qb, cx * 4, cz, at_z),
            ):
                for cp in first:
                    cp.wait_recv()
                for n, d in enumerate((1, 3, 2)):
                    j = lax.rem(own + d, 4)
                    total = sx[i, base + j].astype(F32)
                    for m in range(3):
                        total = total + rx[i, m, j].astype(F32)
                    tx[i, n] = total
                    second.append(copies.start(tx.at[i, n], qx.at[i, n], at(d)))
            return second

        def end(second):
            finish(second)
            halves = []
            for sx, rx, qx, base, own in (
                (sa, ra, qa, cz * 4, cx), (sb, rb, qb, cx * 4, cz),
            ):
                total = sx[i, base + own].astype(F32)
                for m in range(3):
                    total = total + rx[i, m, own].astype(F32)
                for m in range(3):
                    total = total + qx[i, m]
                halves.append(total)
            return jnp.concatenate(halves, axis=1)

        return middle, end

    def entity_gather(i, values=None):
        own = pl.ds(row * 2, 2)
        for n in range(2):
            gy[i][row * 2 + n] = values[n]
        first = [copies.start(gy[i].at[own], gy[i].at[own], at_y(d)) for d in (1, 3, 2)]
        second = [copies.start(gy[i].at[own], gy[i].at[own], mate)]

        def middle():
            for cp, d in zip(first, (1, 3, 2)):
                cp.wait_recv()
                came = pl.ds((lax.rem(cy + 4 - d, 4) * 2 + cc) * 2, 2)
                second.append(copies.start(gy[i].at[came], gy[i].at[came], mate))
            return second

        return middle

    def entity_spread(i):
        for e in range(NB):
            owner = e // 2
            se[i, (owner % 2) * 4 + owner // 2, e % 2] = run[plan[E_LAST, e] + 1]
        first = []
        for n, d in enumerate((1, 3, 2, 0)):
            there = (1 - cc) * 4 + lax.rem(cy + d, 4)
            first.append(copies.start(se.at[i, there], me.at[i, n], mate))

        def middle():
            second = []
            for n, d in enumerate((1, 3, 2)):
                first[n].wait_recv()
                here = cc * 4 + lax.rem(cy + d, 4)
                for m in range(2):
                    te[i, n, m] = (se[i, here, m] + me[i, n, m]).astype(BF16)
                second.append(copies.start(te.at[i, n], qe.at[i, n], at_y(d)))
            first[3].wait_recv()
            return second

        def end(second):
            finish(second)
            here = cc * 4 + cy
            parts = []
            for m in range(2):
                total = se[i, here, m] + me[i, 3, m]
                for n in range(3):
                    total = total + qe[i, n, m].astype(F32)
                parts.append(total)
            return parts

        return middle, end

    nt = (((1,), (1,)), ((), ()))
    nn = (((1,), (0,)), ((), ()))

    def tiles(load_row, load_pair, wx, sx, rows, mode):
        tile_row, keep_row = rows

        def body(q, carry):
            weights, products, pairs = [], [], []
            for u in range(STEP):
                p = q * STEP + u
                mine = load_row(2 * p)
                pair = load_pair(p)
                products.append(lax.dot_general(mine, pair, nt, preferred_element_type=F32))
                pairs.append(pair)
            errors = []
            for u in range(STEP):
                p = q * STEP + u
                t0, t1 = plan[tile_row, 2 * p], plan[tile_row, 2 * p + 1]
                weight = jnp.concatenate([wx[t0], wx[t1]], axis=1).astype(F32)
                if mode == "resid":
                    score = jnp.concatenate([sx[t0], sx[t1]], axis=1).astype(F32)
                    errors.append((weight * (score - products[u])).astype(BF16))
                elif mode == "image":
                    errors.append((weight * products[u]).astype(BF16))
                else:
                    errors.append(weight * products[u] * products[u])
            for u in range(STEP):
                p = q * STEP + u
                keep = plan[keep_row, 2 * p].astype(F32)
                if mode == "curve":
                    term = errors[u][:, :B] + errors[u][:, B:]
                    run_c[p + 1] = run_c[p] * keep + term
                else:
                    term = lax.dot_general(errors[u], pairs[u], nn, preferred_element_type=F32)
                    run[p + 1] = run[p] * keep + term
            return carry

        lax.fori_loop(0, PAIRS // STEP, body, 0)

    def alias_tiles(i, mode):
        def load_row(n):
            return jnp.concatenate([ga[i][plan[A_SWAP, n]], gb[i][plan[A_KEY, n]]], axis=1)

        def load_pair(p):
            e0, e1 = plan[A_OTHER, 2 * p], plan[A_OTHER, 2 * p + 1]
            return jnp.concatenate([gy[0][e0], gy[0][e1]], axis=0)

        tiles(load_row, load_pair, w, s, (A_TILE, A_KEEP), mode)

    def entity_tiles(i, mode):
        def load_row(n):
            return gy[i][plan[E_KEY, n]]

        def load_pair(p):
            a0, a1 = plan[E_OTHER, 2 * p], plan[E_OTHER, 2 * p + 1]
            return jnp.concatenate([xn[a0], xn[a1]], axis=0)

        tiles(load_row, load_pair, wt, st, (E_TILE, E_KEEP), mode)

    def flip(source, target, low, high):
        def body(n, carry):
            for u in range(2):
                target[low + 2 * n + u] = source[low + 2 * n + u].T
            return carry

        lax.fori_loop(0, (high - low) // 2, body, 0)

    def curve_row(last):
        block = run_c[last + 1]
        high = block.astype(BF16)
        low = (block - high.astype(F32)).astype(BF16)
        ones = jnp.ones((16, B), BF16)
        total = lax.dot_general(ones, high, nt, preferred_element_type=F32)
        total = total + lax.dot_general(ones, low, nt, preferred_element_type=F32)
        return total[0:1]

    def first_step(x, r, image_of):
        d = r
        rr = jnp.sum(r * r, axis=-1, keepdims=True)
        image = image_of + ridge * d
        step = rr / (jnp.sum(d * image, axis=-1, keepdims=True) + eps)
        x = x + step * d
        r = r - step * image
        new = jnp.sum(r * r, axis=-1, keepdims=True)
        d = r + (new / (rr + eps)) * d
        return x, d, new

    x0 = x_in[...]
    mid_x = alias_gather(0, x0)
    mid_y = entity_gather(0, [y_in[pl.ds(0, B), :], y_in[pl.ds(B, B), :]])
    zero = jnp.zeros((B, B), BF16)
    for ref in (w, s, wt, st):
        ref[T] = zero
    run[0] = jnp.zeros((B, K), F32)
    run_c[0] = jnp.zeros((B, B), F32)
    second_x = mid_x()
    second_y = mid_y()
    load_w.wait()
    load_s.wait()
    flip(w, wt, 0, 32)
    finish(second_x)
    finish(second_y)
    alias_tiles(0, "resid")
    middle, end = alias_spread(0)
    flip(w, wt, 32, 64)
    second = middle()
    image = end(second)
    vx[...] = x_in[...].astype(F32)
    vr[...] = image - ridge * vx[...]
    mid = alias_gather(1, vr[...].astype(BF16))
    second = mid()
    flip(w, wt, 64, 96)
    finish(second)
    alias_tiles(1, "image")
    middle, end = alias_spread(1)
    flip(s, st, 0, 32)
    second = middle()
    image = end(second)
    x1, d1, rr1 = first_step(vx[...], vr[...], image)
    vd[...] = d1
    vx[...] = x1
    own_rr = to_row(rr1)
    own_dd = ridge * to_row(jnp.sum(d1 * d1, axis=-1, keepdims=True))
    mid = alias_gather(2, vd[...].astype(BF16))
    second = mid()
    mid_x = alias_gather(3, vx[...].astype(BF16))
    flip(s, st, 32, 64)
    finish(second)
    second_x = mid_x()
    alias_tiles(2, "curve")
    for b in range(NB):
        line = curve_row(plan[A_LAST, b])
        cmsg[col, pl.ds(b, 1), :] = line + jnp.where(col == b, own_dd, 0.0)
    cmsg[col, pl.ds(NB, 8), :] = jnp.broadcast_to(own_rr, (8, B))
    small = [
        copies.start(cmsg.at[col], cmsg.at[col], (row, lax.rem(col + d, 16))) for d in range(1, 16)
    ]
    flip(s, st, 64, 96)
    finish(second_x)
    finish(small)
    total = cmsg[0, pl.ds(0, NB), :]
    for b in range(1, NB):
        total = total + cmsg[b, pl.ds(0, NB), :]
    for b in range(NB):
        step = to_column(cmsg[b, pl.ds(NB, 1), :] / (total[b : b + 1] + eps))
        a_slot = (b % 4) * 4 + b // 4
        left = ga[3][a_slot].astype(F32) + step * ga[2][a_slot].astype(F32)
        right = gb[3][b].astype(F32) + step * gb[2][b].astype(F32)
        xn[b] = jnp.concatenate([left, right], axis=1).astype(BF16)
    mine = jnp.sum(
        jnp.where(lax.broadcasted_iota(jnp.int32, (NB, B), 0) == col, total, 0.0),
        axis=0, keepdims=True,
    )
    step = to_column(cmsg[col, pl.ds(NB, 1), :] / (mine + eps))
    x_out[...] = (vx[...] + step * vd[...]).astype(BF16)

    entity_tiles(0, "resid")
    middle, end = entity_spread(0)
    second = middle()
    parts = end(second)
    for m in range(2):
        ux[m] = y_in[pl.ds(m * B, B), :].astype(F32)
        ur[m] = parts[m] - ridge * ux[m]
    mid = entity_gather(1, [ur[m].astype(BF16) for m in range(2)])
    finish(mid())
    entity_tiles(1, "image")
    middle, end = entity_spread(1)
    second = middle()
    parts = end(second)
    norms, dots = [], []
    for m in range(2):
        y1, d1, rr1 = first_step(ux[m], ur[m], parts[m])
        ux[m] = y1
        ud[m] = d1
        norms.append(rr1)
        dots.append(ridge * jnp.sum(d1 * d1, axis=-1, keepdims=True))
    mid = entity_gather(2, [ud[m].astype(BF16) for m in range(2)])
    finish(mid())
    entity_tiles(2, "curve")
    for e in range(NB):
        emsg[0, e // 2, pl.ds(e % 2, 1), :] = curve_row(plan[E_LAST, e])
    small = []
    for d in range(1, 8):
        there = lax.rem(row + d, 8)
        small.append(copies.start(emsg.at[0, there], emsg.at[1, row], (there, col)))
    emsg[1, row] = emsg[0, row]
    finish(small)
    total = emsg[1, 0]
    for n in range(1, 8):
        total = total + emsg[1, n]
    for m in range(2):
        step = norms[m] / (to_column(total[m : m + 1]) + dots[m] + eps)
        y_out[pl.ds(m * B, B), :] = (ux[m] + step * ud[m]).astype(BF16)
    for cp in copies.all:
        cp.wait_send()


def on_device(alias_factors, entity_factors, tile_ids, tile_score, tile_weight):
    plan = pl.pallas_call(
        plan_kernel,
        name="tile_plan",
        out_shape=jax.ShapeDtypeStruct((16, 128), jnp.int32),
    )(tile_ids.reshape(T, 2))
    vmem = pl.BlockSpec(memory_space=pltpu.VMEM)
    hbm = pl.BlockSpec(memory_space=pl.ANY)
    V = pltpu.VMEM
    return pl.pallas_call(
        sweep_kernel,
        name="als_sweep",
        out_shape=(
            jax.ShapeDtypeStruct((B, K), BF16),
            jax.ShapeDtypeStruct((2 * B, K), BF16),
        ),
        in_specs=[pl.BlockSpec(memory_space=pltpu.SMEM), vmem, vmem, hbm, hbm],
        out_specs=(vmem, vmem),
        scratch_shapes=[
            V((T + 1, B, B), BF16), V((T + 1, B, B), BF16),
            V((T + 1, B, B), BF16), V((T + 1, B, B), BF16),
            V((NB, B, K), BF16),
            V((PAIRS + 1, B, K), F32), V((PAIRS + 1, B, B), F32),
            [V((NB, B, B), BF16)] * 4, [V((NB, B, B), BF16)] * 4, [V((NB, B, K), BF16)] * 3,
            V((2, NB, B, B), BF16), V((2, NB, B, B), BF16),
            V((2, 3, 4, B, B), BF16), V((2, 3, 4, B, B), BF16),
            V((2, 3, B, B), F32), V((2, 3, B, B), F32),
            V((2, 3, B, B), F32), V((2, 3, B, B), F32),
            V((2, 8, 2, B, K), F32), V((2, 4, 2, B, K), F32),
            V((2, 3, 2, B, K), BF16), V((2, 3, 2, B, K), BF16),
            V((NB, NB + 8, B), F32), V((2, 8, 8, B), F32),
            V((B, K), F32), V((B, K), F32), V((B, K), F32),
            V((2, B, K), F32), V((2, B, K), F32), V((2, B, K), F32),
            pltpu.SemaphoreType.DMA((N_COPIES,)),
            pltpu.SemaphoreType.DMA((N_COPIES,)),
            pltpu.SemaphoreType.DMA((2,)),
        ],
        compiler_params=pltpu.CompilerParams(
            collective_id=0, has_side_effects=True, vmem_limit_bytes=60 * 2**20
        ),
    )(plan, alias_factors, entity_factors, tile_weight, tile_score)


def solution(mesh):
    placed = (
        P(("row", "col"), None),
        P(("row", "col"), None),
        P("row", "col", None, None),
        P("row", "col", None, None, None),
        P("row", "col", None, None, None),
    )
    return jax.shard_map(
        on_device,
        mesh=mesh,
        in_specs=placed,
        out_specs=(P(("row", "col"), None), P(("row", "col"), None)),
        check_vma=False,
    )
```

time: 841 us -> 162 us (0.19); the launches traced: 827 us -> 160 us
  waiting for transfers between devices: 560 us -> 0 us
  matrix products: 173 us -> 0 us
  Pallas kernels: 0 us -> 155 us
  local copies, waits for them, and re-layouts: 67.3 us -> 4.44 us
  between operations: 14.2 us -> 0.64 us
  other arithmetic: 11.9 us -> 0 us
    reduce_scatter x6 -> x0, waiting for transfers between devices: 322 us -> none  [the longest x3 222 us: alias_share(): lax.psum_scatter(partial_value, 'col', scatter_dimension=0, tiled=True)]
    all_gather x7 -> x0, waiting for transfers between devices: 237 us -> none  [the longest x2 85.8 us: on_device(): lax.all_gather(direction_bf, 'col', axis=0, tiled=True)]
    dot_general x12 -> x0, matrix products: 173 us -> none  [the longest x6 92.2 us: collect(): jnp.einsum('at,tpk->apk', onehot, terms, precision=lax.Precision.HIGHEST)]
    pallas_call x0 -> x2, Pallas kernels: none -> 155 us  [the longest x1 154 us: on_device(): pl.pallas_call(sweep_kernel, name='als_sweep', out_shape=(jax.ShapeDtypeS...]
    gather x7 -> x0, local copies, waits for them, and re-layouts: 51.1 us -> none  [the longest x3 21.6 us: alias_terms(): alias_t = jnp.take(alias_vec, alias_ids, axis=0)]
    dot_general x6 -> x0, local copies, waits for them, and re-layouts: 15.4 us -> none  [collect(): jnp.einsum('at,tpk->apk', onehot, terms, precision=lax.Precision.HIGHEST)]
  transfers between devices with their start and end apart: 13 -> 0, of which waited for: 13 -> 0; matrix products, arithmetic and copies ran while one was open for 1% -> 0% of each run, Pallas kernels for 0% -> 0%
where the time goes in v1:
time: 162 us; the launch traced here: 160 us
  Pallas kernels  155 us (96%)
  local copies, waits for them, and re-layouts  4.44 us (3%)
    pallas_call x1, Pallas kernels, on_device(): pl.pallas_call(sweep_kernel, name='als_sweep', out_shape=(jax.ShapeDtypeS...  154 us
    unnamed x3, local copies, waits for them, and re-layouts  4.44 us

profile of v1, /device:TPU:0, one launch (start us, length us, event | category | flops | bytes accessed | tf_op | source)
XLA Modules:
  0.0 160.4 jit_solution(469493800973163782)
XLA Ops:
  0.6 1.4 copy.7
  2.0 1.8 %tile_plan.1.plan = s32[16,128]{1,0:T(8,128)} custom-call(s32[96,2]{1,0:T(8,128)} %bitcast.1), custom_call_target="tpu_custom_call" | custom-call | tf_op jit(solution)/shard_map/tile_plan/pallas_call | solution.py:455
  3.8 153.5 %als_sweep.1 = (bf16[128,256]{1,0:T(8,128)(2,1)}, bf16[256,256]{1,0:T(8,128)(2,1)}) custom-call(s32[16,128]{1,0:T(8,128)} %tile_plan.1.plan, bf16[128,256]{1,0:T(8,128)(2,1)} %x_in.1, bf16[256,256]{1,0:T(8,128)(2,1)} %y_in.1, bf16[1,1,96,128,128]{4,3,2,1,0:T(8,128)(2,1)} %w_hbm.1, bf16[1,1,96,128,128]{4,3,2,1,0:T(8,128)(2,1)} %s_hbm.1), custom_call_target="tpu_custom_call" | custom-call | tf_op jit(solution)/shard_map/als_sweep/pallas_call | solution.py:463
  157.3 1.5 copy.10
  158.8 1.6 copy.11

commit v2 on v1

v2 whole, which is shorter than its diff:
```python
import functools

import jax
import jax.numpy as jnp
from jax import lax
from jax.experimental import pallas as pl
from jax.experimental.pallas import tpu as pltpu
from jax.sharding import PartitionSpec as P

ridge = 1.0
eps = 1e-06
MESH = pl.DeviceIdType.MESH
F32 = jnp.float32
BF16 = jnp.bfloat16
B = 128
K = 256
T = 96
NB = 16
PAIRS = (T + NB) // 2
STEP = 28
NS = 2
R = B // NS
CHUNKS = ((0, 4),)
PRE = True
THROTTLE = False

A_TILE, A_OTHER, A_KEY, A_SWAP, A_KEEP, A_LAST = range(6)
E_TILE, E_OTHER, E_KEY, E_KEEP, E_LAST = range(6, 11)


def plan_kernel(ids_ref, out_ref):
    ids = ids_ref[...].astype(F32)
    row_i = lax.broadcasted_iota(jnp.int32, (T, 128), 0).astype(F32)
    lane_i = lax.broadcasted_iota(jnp.int32, (T, 128), 1).astype(F32)
    row_t = lax.broadcasted_iota(jnp.int32, (T, T), 0).astype(F32)
    lane_t = lax.broadcasted_iota(jnp.int32, (T, T), 1).astype(F32)
    col = lax.axis_index("col")
    cx, cz = (col // 4).astype(F32), (col % 4).astype(F32)
    out_ref[...] = jnp.zeros_like(out_ref)

    def put(row, value):
        out_ref[row : row + 1, :] = value.astype(jnp.int32)

    lines = [jnp.broadcast_to(ids[n : n + 1, :], (T, T)) for n in range(2)]
    columns = [
        jnp.sum(jnp.where(row_t == lane_t, line, 0.0), axis=1, keepdims=True) for line in lines
    ]
    for key, rows in (
        (0, (A_TILE, A_OTHER, A_KEY, A_KEEP, A_LAST)),
        (1, (E_TILE, E_OTHER, E_KEY, E_KEEP, E_LAST)),
    ):
        kc = jnp.broadcast_to(columns[key], (T, 128))
        oc = jnp.broadcast_to(columns[1 - key], (T, 128))
        same = jnp.where(jnp.broadcast_to(columns[key], (T, T)) == lines[key], 1.0, 0.0)
        rank = jnp.sum(jnp.where(lane_t < row_t, same, 0.0), axis=1, keepdims=True)
        count = jnp.sum(same, axis=1, keepdims=True)
        odd = count - 2.0 * jnp.floor(count * 0.5)
        width = jnp.broadcast_to(1.0 + jnp.where(rank == 0.0, odd, 0.0), (T, 128))
        n_row = jnp.sum(jnp.where(kc == lane_i, width, 0.0), axis=0, keepdims=True)
        start = jnp.sum(
            jnp.where(lane_i < kc, jnp.broadcast_to(n_row, (T, 128)), 0.0), axis=1, keepdims=True
        )
        pos = jnp.broadcast_to(start + rank, (T, 128))
        hit = jnp.where(pos == lane_i, 1.0, 0.0)
        valid = jnp.sum(hit, axis=0, keepdims=True)
        put(rows[0], jnp.sum(hit * row_i, axis=0, keepdims=True) + T * (1.0 - valid))
        put(rows[1], jnp.sum(hit * oc, axis=0, keepdims=True))
        key_row = jnp.sum(hit * kc, axis=0, keepdims=True)
        if key == 0:
            high = jnp.floor(key_row * 0.25)
            low = key_row - 4.0 * high
            put(A_KEY, high * 4.0 + low - cz + jnp.where(low < cz, 4.0, 0.0))
            put(A_SWAP, low * 4.0 + high - cx + jnp.where(high < cx, 4.0, 0.0))
        else:
            put(rows[2], key_row)
        keep = jnp.where(jnp.broadcast_to(rank, (T, 128)) > 0.0, hit, 0.0)
        put(rows[3], jnp.sum(keep, axis=0, keepdims=True))
        upto = jnp.sum(jnp.where(kc <= lane_i, width, 0.0), axis=0, keepdims=True)
        put(rows[4], upto * 0.5 - 1.0)


class Copies:
    def __init__(self, send, recv):
        self.send, self.recv, self.all, self.done, self.batch = send, recv, [], [], []

    def start(self, src, dst, device):
        n = len(self.all)
        cp = pltpu.make_async_remote_copy(
            src_ref=src,
            dst_ref=dst,
            send_sem=self.send.at[n],
            recv_sem=self.recv.at[n],
            device_id=device,
            device_id_type=MESH,
        )
        cp.start()
        self.all.append(cp)
        return cp

    def flush(self, some):
        for cp in some:
            if not any(cp is other for other in self.done):
                cp.wait_send()
                self.done.append(cp)

    def turn(self, batch):
        if THROTTLE:
            self.flush(self.batch)
        self.batch = batch
        return batch


N_GATHER = 18 if PRE else 12
N_COPIES = NS * (N_GATHER * 4 + (6 * len(CHUNKS) + 6) * 2 + 7 * 2 + 7 * 2) + 7 + 15 + 7
FAR = (1, 3, 2)


def sweep_kernel(
    plan, x_in, y_in, w_hbm, s_hbm, x_out, y_out,
    w, s, wt, st, xn, run, run_c, ga, gb, gy0, gy, sa, sb, ra, rb, ta, tb, qa, qb,
    se, me, te, qe, cmsg, emsg, vx, vr, vd, vn, vq, ux, ur, ud, un, uq,
    send, recv, lsem,
):
    row = lax.axis_index("row")
    col = lax.axis_index("col")
    cy, cc = row // 2, row % 2
    cx, cz = col // 4, col % 4

    def at_x(d):
        return (row, lax.rem(cx + d, 4) * 4 + cz)

    def at_z(d):
        return (row, cx * 4 + lax.rem(cz + d, 4))

    def at_y(d):
        return (lax.rem(cy + d, 4) * 2 + cc, col)

    mate = (cy * 2 + (1 - cc), col)

    copies = Copies(send, recv)
    load_w = pltpu.make_async_copy(w_hbm.at[0, 0], w.at[pl.ds(0, T)], lsem.at[0])
    load_s = pltpu.make_async_copy(s_hbm.at[0, 0], s.at[pl.ds(0, T)], lsem.at[1])
    load_w.start()
    load_s.start()

    barrier = pltpu.get_barrier_semaphore()
    for d in range(1, 16):
        pl.semaphore_signal(barrier, 1, device_id=(row, lax.rem(col + d, 16)), device_id_type=MESH)
    for d in range(1, 8):
        pl.semaphore_signal(barrier, 1, device_id=(lax.rem(row + d, 8), col), device_id_type=MESH)
    pl.semaphore_wait(barrier, 22)

    eye = jnp.where(
        lax.broadcasted_iota(jnp.int32, (B, B), 0) == lax.broadcasted_iota(jnp.int32, (B, B), 1),
        1.0, 0.0,
    ).astype(F32)

    def to_row(column):
        return jnp.sum(jnp.broadcast_to(column, (B, B)) * eye, axis=0, keepdims=True)

    def to_column(line):
        return jnp.sum(jnp.broadcast_to(line, (B, B)) * eye, axis=1, keepdims=True)

    def arrived(list_of_copies):
        for cp in list_of_copies:
            cp.wait_recv()

    def alias_gather(i, h, value):
        a, b = ga[i][h], gb[i][h]
        a[cz * 4] = value[:, :B]
        b[cx * 4] = value[:, B:]
        first_a, first_b, second = [], [], []
        for d in FAR:
            first_a.append(copies.start(a.at[cz * 4], a.at[cz * 4 + 4 - d], at_x(d)))
            first_b.append(copies.start(b.at[cx * 4], b.at[cx * 4 + 4 - d], at_z(d)))
        if PRE:
            for d in FAR:
                second.append(copies.start(a.at[cz * 4], a.at[cz * 4], at_z(d)))
                second.append(copies.start(b.at[cx * 4], b.at[cx * 4], at_x(d)))
        skip = 1 if PRE else 0

        def middle():
            arrived(first_a + first_b)
            batch = copies.turn([])
            for ref, base, at in ((a, cz * 4, at_z), (b, cx * 4, at_x)):
                rows = pl.ds(base + skip, 4 - skip)
                for d in FAR:
                    batch.append(copies.start(ref.at[rows], ref.at[rows], at(d)))
            return second + batch

        return middle

    def alias_spread(i, h):
        halves = (
            (sa[i][h], ra[i][h], ta[i][h], qa[i][h], cx, cz, at_x, at_z),
            (sb[i][h], rb[i][h], tb[i][h], qb[i][h], cz, cx, at_z, at_x),
        )
        firsts = [[], []]
        for low, high in CHUNKS:
            for k, (sx, rx, tx, qx, near, far, at_near, at_far) in enumerate(halves):
                for m in range(4):
                    for pos in range(low, high):
                        other = lax.rem(near + 3 - pos, 4)
                        block = other * 4 + m if k == 0 else m * 4 + other
                        part = run[plan[A_LAST, block] + 1, h * R : (h + 1) * R, k * B : (k + 1) * B]
                        sx[m, pos] = part.astype(BF16)
            batch = copies.turn([])
            for k, (sx, rx, tx, qx, near, far, at_near, at_far) in enumerate(halves):
                span = pl.ds(low, high - low)
                firsts[k].append(
                    [
                        copies.start(sx.at[lax.rem(far + d, 4), span], rx.at[n, span], at_far(d))
                        for n, d in enumerate(FAR)
                    ]
                )
                batch.extend(firsts[k][-1])

        def middle():
            second = []
            for c, (low, high) in enumerate(CHUNKS):
                for k, (sx, rx, tx, qx, near, far, at_near, at_far) in enumerate(halves):
                    arrived(firsts[k][c])
                    for pos in range(low, min(high, 3)):
                        total = sx[far, pos].astype(F32)
                        for n in range(3):
                            total = total + rx[n, pos].astype(F32)
                        tx[pos] = total.astype(BF16)
                        second.append(copies.start(tx.at[pos], qx.at[pos], at_near(3 - pos)))
            return second

        def end(second):
            arrived(second)
            sums = []
            for sx, rx, tx, qx, near, far, at_near, at_far in halves:
                total = sx[far, 3].astype(F32)
                for n in range(3):
                    total = total + rx[n, 3].astype(F32)
                for n in range(3):
                    total = total + qx[n].astype(F32)
                sums.append(total)
            return jnp.concatenate(sums, axis=1)

        return middle, end

    def entity_gather(ref, values):
        own = pl.ds(row * 2, 2)
        for n in range(2):
            ref[row * 2 + n] = values[n]
        first = copies.turn([])
        first.extend([copies.start(ref.at[own], ref.at[own], at_y(d)) for d in FAR])
        second = [copies.start(ref.at[own], ref.at[own], mate)]

        def middle():
            for cp, d in zip(first, FAR):
                cp.wait_recv()
                came = pl.ds((lax.rem(cy + 4 - d, 4) * 2 + cc) * 2, 2)
                second.append(copies.start(ref.at[came], ref.at[came], mate))
            return second

        return middle

    def entity_spread(i, h):
        sx, mx, tx, qx = se[i][h], me[i][h], te[i][h], qe[i][h]
        first = []
        for n, d in enumerate(FAR + (0,)):
            y = lax.rem(cy + d, 4)
            for c in range(2):
                for m in range(2):
                    sx[c, n, m] = run[plan[E_LAST, (y * 2 + c) * 2 + m] + 1, h * R : (h + 1) * R]
            first.append(copies.start(sx.at[1 - cc, n], mx.at[n], mate))

        def middle():
            second = copies.turn([])
            for n, d in enumerate(FAR):
                first[n].wait_recv()
                for m in range(2):
                    tx[n, m] = (sx[cc, n, m] + mx[n, m]).astype(BF16)
                second.append(copies.start(tx.at[n], qx.at[n], at_y(d)))
            first[3].wait_recv()
            return second

        def end(second):
            arrived(second)
            parts = []
            for m in range(2):
                total = sx[cc, 3, m] + mx[3, m]
                for n in range(3):
                    total = total + qx[n, m].astype(F32)
                parts.append(total)
            return parts

        return middle, end

    nt = (((1,), (1,)), ((), ()))
    nn = (((1,), (0,)), ((), ()))

    def tiles(load_row, load_pair, wx, sx, rows, mode):
        tile_row, keep_row = rows

        def body(q, carry):
            products, pairs, errors = [], [], []
            for u in range(STEP):
                p = q * STEP + u
                mine = load_row(2 * p)
                pair = load_pair(p)
                products.append(lax.dot_general(mine, pair, nt, preferred_element_type=F32))
                pairs.append(pair)
            for u in range(STEP):
                p = q * STEP + u
                t0, t1 = plan[tile_row, 2 * p], plan[tile_row, 2 * p + 1]
                weight = jnp.concatenate([wx[t0], wx[t1]], axis=1).astype(F32)
                if mode == "resid":
                    score = jnp.concatenate([sx[t0], sx[t1]], axis=1).astype(F32)
                    errors.append((weight * (score - products[u])).astype(BF16))
                elif mode == "image":
                    errors.append((weight * products[u]).astype(BF16))
                else:
                    errors.append(weight * products[u] * products[u])
            for u in range(STEP):
                p = q * STEP + u
                keep = plan[keep_row, 2 * p].astype(F32)
                if mode == "curve":
                    term = errors[u][:, :B] + errors[u][:, B:]
                    run_c[p + 1] = run_c[p] * keep + term
                else:
                    term = lax.dot_general(errors[u], pairs[u], nn, preferred_element_type=F32)
                    run[p + 1] = run[p] * keep + term
            return carry

        lax.fori_loop(0, PAIRS // STEP, body, 0)

    def alias_tiles(i, mode):
        def load_row(n):
            left = jnp.concatenate([ga[i][h][plan[A_SWAP, n]] for h in range(NS)], axis=0)
            right = jnp.concatenate([gb[i][h][plan[A_KEY, n]] for h in range(NS)], axis=0)
            return jnp.concatenate([left, right], axis=1)

        def load_pair(p):
            e0, e1 = plan[A_OTHER, 2 * p], plan[A_OTHER, 2 * p + 1]
            return jnp.concatenate([gy0[e0], gy0[e1]], axis=0)

        tiles(load_row, load_pair, w, s, (A_TILE, A_KEEP), mode)

    def entity_tiles(i, mode):
        def load_row(n):
            if i == 0:
                return gy0[plan[E_KEY, n]]
            return jnp.concatenate([gy[i - 1][h][plan[E_KEY, n]] for h in range(NS)], axis=0)

        def load_pair(p):
            a0, a1 = plan[E_OTHER, 2 * p], plan[E_OTHER, 2 * p + 1]
            return jnp.concatenate([xn[a0], xn[a1]], axis=0)

        tiles(load_row, load_pair, wt, st, (E_TILE, E_KEEP), mode)

    def flip(source, target, low, high):
        def body(n, carry):
            for u in range(4):
                target[low + 4 * n + u] = source[low + 4 * n + u].T
            return carry

        lax.fori_loop(0, (high - low) // 4, body, 0)

    def curve_row(last):
        block = run_c[last + 1]
        high = block.astype(BF16)
        low = (block - high.astype(F32)).astype(BF16)
        ones = jnp.ones((16, B), BF16)
        total = lax.dot_general(ones, high, nt, preferred_element_type=F32)
        total = total + lax.dot_general(ones, low, nt, preferred_element_type=F32)
        return total[0:1]

    def first_step(x, r, image_of):
        d = r
        rr = jnp.sum(r * r, axis=-1, keepdims=True)
        image = image_of + ridge * d
        step = rr / (jnp.sum(d * image, axis=-1, keepdims=True) + eps)
        x = x + step * d
        r = r - step * image
        new = jnp.sum(r * r, axis=-1, keepdims=True)
        d = r + (new / (rr + eps)) * d
        return x, d, new

    flips = [
        (src, dst, n, n + 16) for src, dst in ((w, wt), (s, st)) for n in range(0, T, 16)
    ]

    def together(streams):
        streams = list(streams)
        while streams:
            for stream in list(streams):
                try:
                    next(stream)
                except StopIteration:
                    streams.remove(stream)

    def gap():
        for n in range(3):
            if flips:
                flip(*flips.pop(0))

    y_gather = []

    def alias_stream(h):
        rows = pl.ds(h * R, R)
        x0 = x_in[rows, :]
        mid = alias_gather(0, h, x0)
        if h == 0:
            mid_y = entity_gather(gy0, [y_in[pl.ds(0, B), :], y_in[pl.ds(B, B), :]])
        yield
        second = mid()
        if h == 0:
            y_gather.append(mid_y())
            load_w.wait()
            load_s.wait()
            zero = jnp.zeros((B, B), BF16)
            for ref in (w, s, wt, st):
                ref[T] = zero
            run[0] = jnp.zeros((B, K), F32)
            run_c[0] = jnp.zeros((B, B), F32)
        if h == NS - 1:
            gap()
        yield
        arrived(second)
        if h == NS - 1:
            arrived(y_gather[0])
            alias_tiles(0, "resid")
        yield
        middle, end = alias_spread(0, h)
        if h == NS - 1:
            gap()
        yield
        second = middle()
        yield
        image = end(second)
        x = x_in[rows, :].astype(F32)
        r = image - ridge * x
        vr[rows, :] = r
        mid = alias_gather(1, h, r.astype(BF16))
        yield
        second = mid()
        if h == NS - 1:
            gap()
        yield
        arrived(second)
        if h == NS - 1:
            alias_tiles(1, "image")
        yield
        middle, end = alias_spread(1, h)
        if h == NS - 1:
            gap()
        yield
        second = middle()
        yield
        image = end(second)
        x1, d1, rr1 = first_step(x_in[rows, :].astype(F32), vr[rows, :], image)
        mid = alias_gather(2, h, d1.astype(BF16))
        vd[rows, :] = d1
        vx[rows, :] = x1
        vn[rows, :] = jnp.broadcast_to(rr1, (R, B))
        vq[rows, :] = jnp.broadcast_to(ridge * jnp.sum(d1 * d1, axis=-1, keepdims=True), (R, B))
        yield
        second = mid()
        if h == NS - 1:
            gap()
        yield
        mid_x = alias_gather(3, h, vx[rows, :].astype(BF16))
        arrived(second)
        yield
        x_gather.extend(mid_x())
        if h == NS - 1:
            alias_tiles(2, "curve")

    x_gather = []
    together([alias_stream(h) for h in range(NS)])
    while flips:
        flip(*flips.pop(0))
    own_dd = jnp.sum(vq[...] * eye, axis=0, keepdims=True)
    own_rr = jnp.sum(vn[...] * eye, axis=0, keepdims=True)
    for b in range(NB):
        line = curve_row(plan[A_LAST, b])
        cmsg[col, pl.ds(b, 1), :] = line + jnp.where(col == b, own_dd, 0.0)
    cmsg[col, pl.ds(NB, 8), :] = jnp.broadcast_to(own_rr, (8, B))
    small = [
        copies.start(cmsg.at[col], cmsg.at[col], (row, lax.rem(col + d, 16))) for d in range(1, 16)
    ]
    arrived(x_gather)
    arrived(small)
    total = cmsg[0, pl.ds(0, NB), :]
    for b in range(1, NB):
        total = total + cmsg[b, pl.ds(0, NB), :]
    for b in range(NB):
        step = to_column(cmsg[b, pl.ds(NB, 1), :] / (total[b : b + 1] + eps))
        a_slot = (b % 4) * 4 + lax.rem(b // 4 + 4 - cx, 4)
        b_slot = (b // 4) * 4 + lax.rem(b % 4 + 4 - cz, 4)
        for h in range(NS):
            cut = slice(h * R, (h + 1) * R)
            left = ga[3][h][a_slot].astype(F32) + step[cut] * ga[2][h][a_slot].astype(F32)
            right = gb[3][h][b_slot].astype(F32) + step[cut] * gb[2][h][b_slot].astype(F32)
            xn[b, cut] = jnp.concatenate([left, right], axis=1).astype(BF16)

    def entity_stream(h):
        halves = [pl.ds(m * B + h * R, R) for m in range(2)]
        if h == 0:
            entity_tiles(0, "resid")
        middle, end = entity_spread(0, h)
        yield
        second = middle()
        yield
        parts = end(second)
        rs = [parts[m] - ridge * y_in[halves[m], :].astype(F32) for m in range(2)]
        mid = entity_gather(gy[0][h], [r.astype(BF16) for r in rs])
        for m in range(2):
            ur[halves[m], :] = rs[m]
        yield
        second = mid()
        yield
        arrived(second)
        if h == NS - 1:
            entity_tiles(1, "image")
        yield
        middle, end = entity_spread(1, h)
        yield
        second = middle()
        yield
        parts = end(second)
        steps = [
            first_step(y_in[halves[m], :].astype(F32), ur[halves[m], :], parts[m])
            for m in range(2)
        ]
        mid = entity_gather(gy[1][h], [step[1].astype(BF16) for step in steps])
        for m, (y1, d1, rr1) in enumerate(steps):
            ux[halves[m], :] = y1
            ud[halves[m], :] = d1
            un[halves[m], :] = jnp.broadcast_to(rr1, (R, B))
            uq[halves[m], :] = jnp.broadcast_to(
                ridge * jnp.sum(d1 * d1, axis=-1, keepdims=True), (R, B)
            )
        yield
        second = mid()
        yield
        arrived(second)
        if h == NS - 1:
            entity_tiles(2, "curve")

    together([entity_stream(h) for h in range(NS)])
    for e in range(NB):
        emsg[0, e // 2, pl.ds(e % 2, 1), :] = curve_row(plan[E_LAST, e])
    small = []
    for d in range(1, 8):
        there = lax.rem(row + d, 8)
        small.append(copies.start(emsg.at[0, there], emsg.at[1, row], (there, col)))
    emsg[1, row] = emsg[0, row]
    mine = jnp.sum(
        jnp.where(lax.broadcasted_iota(jnp.int32, (NB, B), 0) == col, total, 0.0),
        axis=0, keepdims=True,
    )
    step = to_column(cmsg[col, pl.ds(NB, 1), :] / (mine + eps))
    x_out[...] = (vx[...] + step * vd[...]).astype(BF16)
    arrived(small)
    total = emsg[1, 0]
    for n in range(1, 8):
        total = total + emsg[1, n]
    for m in range(2):
        rows = pl.ds(m * B, B)
        step = un[rows, :][:, :1] / (to_column(total[m : m + 1]) + uq[rows, :][:, :1] + eps)
        y_out[rows, :] = (ux[rows, :] + step * ud[rows, :]).astype(BF16)
    copies.flush(copies.all)


def emit_kernel(x_in, y_in, x_out, y_out):
    x_out[...] = x_in[...]
    y_out[...] = y_in[...]


def on_device(alias_factors, entity_factors, tile_ids, tile_score, tile_weight):
    plan = pl.pallas_call(
        plan_kernel,
        name="tile_plan",
        out_shape=jax.ShapeDtypeStruct((16, 128), jnp.int32),
    )(tile_ids[0, 0].T)
    vmem = pl.BlockSpec(memory_space=pltpu.VMEM)
    hbm = pl.BlockSpec(memory_space=pl.ANY)
    V = pltpu.VMEM

    def each(n, shape, dtype):
        return [[V(shape, dtype) for h in range(NS)] for i in range(n)]

    results = pl.pallas_call(
        sweep_kernel,
        name="als_sweep",
        out_shape=(
            jax.ShapeDtypeStruct((B, K), BF16),
            jax.ShapeDtypeStruct((2 * B, K), BF16),
        ),
        in_specs=[pl.BlockSpec(memory_space=pltpu.SMEM), vmem, vmem, hbm, hbm],
        out_specs=(vmem, vmem),
        scratch_shapes=[
            V((T + 1, B, B), BF16), V((T + 1, B, B), BF16),
            V((T + 1, B, B), BF16), V((T + 1, B, B), BF16),
            V((NB, B, K), BF16),
            V((PAIRS + 1, B, K), F32), V((PAIRS + 1, B, B), F32),
            each(4, (NB, R, B), BF16), each(4, (NB, R, B), BF16),
            V((NB, B, K), BF16), each(2, (NB, R, K), BF16),
            each(2, (4, 4, R, B), BF16), each(2, (4, 4, R, B), BF16),
            each(2, (3, 4, R, B), BF16), each(2, (3, 4, R, B), BF16),
            each(2, (3, R, B), BF16), each(2, (3, R, B), BF16),
            each(2, (3, R, B), BF16), each(2, (3, R, B), BF16),
            each(2, (2, 4, 2, R, K), F32), each(2, (4, 2, R, K), F32),
            each(2, (3, 2, R, K), BF16), each(2, (3, 2, R, K), BF16),
            V((NB, NB + 8, B), F32), V((2, 8, 8, B), F32),
            V((B, K), F32), V((B, K), F32), V((B, K), F32), V((B, B), F32), V((B, B), F32),
            V((2 * B, K), F32), V((2 * B, K), F32), V((2 * B, K), F32),
            V((2 * B, B), F32), V((2 * B, B), F32),
            pltpu.SemaphoreType.DMA((N_COPIES,)),
            pltpu.SemaphoreType.DMA((N_COPIES,)),
            pltpu.SemaphoreType.DMA((2,)),
        ],
        compiler_params=pltpu.CompilerParams(
            collective_id=0, has_side_effects=True, vmem_limit_bytes=60 * 2**20
        ),
    )(plan, alias_factors, entity_factors, tile_weight, tile_score)
    return pl.pallas_call(
        emit_kernel,
        name="emit",
        out_shape=(
            jax.ShapeDtypeStruct((B, K), BF16),
            jax.ShapeDtypeStruct((2 * B, K), BF16),
        ),
    )(*results)


def solution(mesh):
    placed = (
        P(("row", "col"), None),
        P(("row", "col"), None),
        P("row", "col", None, None),
        P("row", "col", None, None, None),
        P("row", "col", None, None, None),
    )
    return jax.shard_map(
        on_device,
        mesh=mesh,
        in_specs=placed,
        out_specs=(P(("row", "col"), None), P(("row", "col"), None)),
        check_vma=False,
    )
```

time: 162 us -> 137 us (0.85)
  Pallas kernels: 155 us -> 135 us
  local copies, waits for them, and re-layouts: 4.44 us -> 0 us
    pallas_call x1, Pallas kernels: 154 us -> 132 us  [on_device(): pl.pallas_call(sweep_kernel, name='als_sweep', out_shape=(jax.ShapeDtypeS...]
    unnamed x3 -> x0, local copies, waits for them, and re-layouts: 4.44 us -> none
    pallas_call x0 -> x1, Pallas kernels: none -> 1.63 us  [on_device(): pl.pallas_call(emit_kernel, name='emit', out_shape=(jax.ShapeDtypeStruct(...]
where the time goes in v2:
time: 137 us; the launch traced here: 136 us
  Pallas kernels  135 us (99%)
    pallas_call x1, Pallas kernels, on_device(): pl.pallas_call(sweep_kernel, name='als_sweep', out_shape=(jax.ShapeDtypeS...  132 us

profile of v2, /device:TPU:0, one launch (start us, length us, event | category | flops | bytes accessed | tf_op | source)
XLA Modules:
  0.0 135.9 jit_solution(10709836669120880298)
XLA Ops:
  0.6 1.6 %tile_plan.1.plan = s32[16,128]{1,0:T(8,128)} custom-call(s32[2,96]{1,0:T(2,128)} %bitcast.3), custom_call_target="tpu_custom_call" | custom-call | tf_op jit(solution)/shard_map/tile_plan/pallas_call | solution.py:577
  2.3 132.0 %als_sweep.1 = (bf16[128,256]{1,0:T(8,128)(2,1)}, bf16[256,256]{1,0:T(8,128)(2,1)}) custom-call(s32[16,128]{1,0:T(8,128)} %tile_plan.1.plan, bf16[128,256]{1,0:T(8,128)(2,1)} %x_in.1, bf16[256,256]{1,0:T(8,128)(2,1)} %y_in.1, bf16[1,1,96,128,128]{4,3,2,1,0:T(8,128)(2,1)} %w_hbm.1, bf16[1,1,96,128,128]{4,3,2,1,0:T(8,128)(2,1)} %s_hbm.1), custom_call_target="tpu_custom_call" | custom-call | tf_op jit(solution)/shard_map/als_sweep/pallas_call | solution.py:589
  134.3 1.6 %emit.1 = (bf16[128,256]{1,0:T(8,128)(2,1)}, bf16[256,256]{1,0:T(8,128)(2,1)}) custom-call(bf16[128,256]{1,0:T(8,128)(2,1)} %get-tuple-element.4.x_in, bf16[256,256]{1,0:T(8,128)(2,1)} %get-tuple-element.5.y_in), custom_call_target="tpu_custom_call" | custom-call | tf_op jit(solution)/shard_map/emit/pallas_call | solution.py:623

commit v3 on v2

--- a/solution.py
+++ b/solution.py
@@ -22,24 +22,24 @@
 R = B // NS
 CHUNKS = ((0, 4),)
 PRE = True
-THROTTLE = False
 
 A_TILE, A_OTHER, A_KEY, A_SWAP, A_KEEP, A_LAST = range(6)
 E_TILE, E_OTHER, E_KEY, E_KEEP, E_LAST = range(6, 11)
-
-
-def plan_kernel(ids_ref, out_ref):
+TOPS = (T, 15, 15, 15, 1, PAIRS - 1, T, 15, 15, 1, PAIRS - 1)
+
+
+def tile_plan(ids_ref, out_ref, cx, cz):
     ids = ids_ref[...].astype(F32)
     row_i = lax.broadcasted_iota(jnp.int32, (T, 128), 0).astype(F32)
     lane_i = lax.broadcasted_iota(jnp.int32, (T, 128), 1).astype(F32)
     row_t = lax.broadcasted_iota(jnp.int32, (T, T), 0).astype(F32)
     lane_t = lax.broadcasted_iota(jnp.int32, (T, T), 1).astype(F32)
-    col = lax.axis_index("col")
-    cx, cz = (col // 4).astype(F32), (col % 4).astype(F32)
+    cx, cz = cx.astype(F32), cz.astype(F32)
     out_ref[...] = jnp.zeros_like(out_ref)
 
     def put(row, value):
-        out_ref[row : row + 1, :] = value.astype(jnp.int32)
+        top = TOPS[row]
+        out_ref[row : row + 1, :] = jnp.minimum(jnp.maximum(value.astype(jnp.int32), 0), top)
 
     lines = [jnp.broadcast_to(ids[n : n + 1, :], (T, T)) for n in range(2)]
     columns = [
@@ -103,23 +103,17 @@
                 cp.wait_send()
                 self.done.append(cp)
 
-    def turn(self, batch):
-        if THROTTLE:
-            self.flush(self.batch)
-        self.batch = batch
-        return batch
-
 
 N_GATHER = 18 if PRE else 12
-N_COPIES = NS * (N_GATHER * 4 + (6 * len(CHUNKS) + 6) * 2 + 7 * 2 + 7 * 2) + 7 + 15 + 7
+N_COPIES = NS * (N_GATHER * 4 + (6 * len(CHUNKS) + 6) * 2 + 7 * 2 + 7 * 2) + 7 + 6 + 4
 FAR = (1, 3, 2)
 
 
 def sweep_kernel(
-    plan, x_in, y_in, w_hbm, s_hbm, x_out, y_out,
+    ids, x_in, y_in, w_hbm, s_hbm, x_out, y_out,
     w, s, wt, st, xn, run, run_c, ga, gb, gy0, gy, sa, sb, ra, rb, ta, tb, qa, qb,
-    se, me, te, qe, cmsg, emsg, vx, vr, vd, vn, vq, ux, ur, ud, un, uq,
-    send, recv, lsem,
+    se, me, te, qe, cmsg, csum, emsg, ecome, esum, elast, vx, vr, vd, vn, vq, ux, ur, ud, un, uq,
+    plan_v, plan, send, recv, lsem,
 ):
     row = lax.axis_index("row")
     col = lax.axis_index("col")
@@ -140,15 +134,14 @@
     copies = Copies(send, recv)
     load_w = pltpu.make_async_copy(w_hbm.at[0, 0], w.at[pl.ds(0, T)], lsem.at[0])
     load_s = pltpu.make_async_copy(s_hbm.at[0, 0], s.at[pl.ds(0, T)], lsem.at[1])
+    load_plan = pltpu.make_async_copy(plan_v, plan, lsem.at[2])
     load_w.start()
     load_s.start()
 
     barrier = pltpu.get_barrier_semaphore()
-    for d in range(1, 16):
-        pl.semaphore_signal(barrier, 1, device_id=(row, lax.rem(col + d, 16)), device_id_type=MESH)
-    for d in range(1, 8):
-        pl.semaphore_signal(barrier, 1, device_id=(lax.rem(row + d, 8), col), device_id_type=MESH)
-    pl.semaphore_wait(barrier, 22)
+    for peer in [at(d) for at in (at_x, at_z, at_y) for d in FAR] + [mate]:
+        pl.semaphore_signal(barrier, 1, device_id=peer, device_id_type=MESH)
+    pl.semaphore_wait(barrier, 10)
 
     eye = jnp.where(
         lax.broadcasted_iota(jnp.int32, (B, B), 0) == lax.broadcasted_iota(jnp.int32, (B, B), 1),
@@ -181,7 +174,7 @@
 
         def middle():
             arrived(first_a + first_b)
-            batch = copies.turn([])
+            batch = []
             for ref, base, at in ((a, cz * 4, at_z), (b, cx * 4, at_x)):
                 rows = pl.ds(base + skip, 4 - skip)
                 for d in FAR:
@@ -204,8 +197,6 @@
                         block = other * 4 + m if k == 0 else m * 4 + other
                         part = run[plan[A_LAST, block] + 1, h * R : (h + 1) * R, k * B : (k + 1) * B]
                         sx[m, pos] = part.astype(BF16)
-            batch = copies.turn([])
-            for k, (sx, rx, tx, qx, near, far, at_near, at_far) in enumerate(halves):
                 span = pl.ds(low, high - low)
                 firsts[k].append(
                     [
@@ -213,7 +204,6 @@
                         for n, d in enumerate(FAR)
                     ]
                 )
-                batch.extend(firsts[k][-1])
 
         def middle():
             second = []
@@ -224,7 +214,7 @@
                         total = sx[far, pos].astype(F32)
                         for n in range(3):
                             total = total + rx[n, pos].astype(F32)
-                        tx[pos] = total.astype(BF16)
+                        tx[pos] = total
                         second.append(copies.start(tx.at[pos], qx.at[pos], at_near(3 - pos)))
             return second
 
@@ -236,7 +226,7 @@
                 for n in range(3):
                     total = total + rx[n, 3].astype(F32)
                 for n in range(3):
-                    total = total + qx[n].astype(F32)
+                    total = total + qx[n]
                 sums.append(total)
             return jnp.concatenate(sums, axis=1)
 
@@ -246,7 +236,7 @@
         own = pl.ds(row * 2, 2)
         for n in range(2):
             ref[row * 2 + n] = values[n]
-        first = copies.turn([])
+        first = []
         first.extend([copies.start(ref.at[own], ref.at[own], at_y(d)) for d in FAR])
         second = [copies.start(ref.at[own], ref.at[own], mate)]
 
@@ -270,7 +260,7 @@
             first.append(copies.start(sx.at[1 - cc, n], mx.at[n], mate))
 
         def middle():
-            second = copies.turn([])
+            second = []
             for n, d in enumerate(FAR):
                 first[n].wait_recv()
                 for m in range(2):
@@ -410,7 +400,10 @@
         yield
         second = mid()
         if h == 0:
+            tile_plan(ids, plan_v, cx, cz)
+            load_plan.start()
             y_gather.append(mid_y())
+            load_plan.wait()
             load_w.wait()
             load_s.wait()
             zero = jnp.zeros((B, B), BF16)
@@ -418,6 +411,7 @@
                 ref[T] = zero
             run[0] = jnp.zeros((B, K), F32)
             run_c[0] = jnp.zeros((B, B), F32)
+            emsg[...] = jnp.zeros_like(emsg)
         if h == NS - 1:
             gap()
         yield
@@ -479,18 +473,17 @@
     own_rr = jnp.sum(vn[...] * eye, axis=0, keepdims=True)
     for b in range(NB):
         line = curve_row(plan[A_LAST, b])
-        cmsg[col, pl.ds(b, 1), :] = line + jnp.where(col == b, own_dd, 0.0)
-    cmsg[col, pl.ds(NB, 8), :] = jnp.broadcast_to(own_rr, (8, B))
-    small = [
-        copies.start(cmsg.at[col], cmsg.at[col], (row, lax.rem(col + d, 16))) for d in range(1, 16)
-    ]
+        cmsg[0, pl.ds(b, 1), :] = line + jnp.where(col == b, own_dd, 0.0)
+        cmsg[0, pl.ds(NB + b, 1), :] = jnp.where(col == b, own_rr, 0.0)
+    arrived([copies.start(cmsg.at[0], cmsg.at[4 - d], at_x(d)) for d in FAR])
+    csum[0] = (cmsg[0] + cmsg[1]) + (cmsg[2] + cmsg[3])
+    small = [copies.start(csum.at[0], csum.at[4 - d], at_z(d)) for d in FAR]
     arrived(x_gather)
     arrived(small)
-    total = cmsg[0, pl.ds(0, NB), :]
-    for b in range(1, NB):
-        total = total + cmsg[b, pl.ds(0, NB), :]
+    total = (csum[0] + csum[1]) + (csum[2] + csum[3])
+    rates = total[NB:] / (total[:NB] + eps)
     for b in range(NB):
-        step = to_column(cmsg[b, pl.ds(NB, 1), :] / (total[b : b + 1] + eps))
+        step = to_column(rates[b : b + 1])
         a_slot = (b % 4) * 4 + lax.rem(b // 4 + 4 - cx, 4)
         b_slot = (b // 4) * 4 + lax.rem(b % 4 + 4 - cz, 4)
         for h in range(NS):
@@ -544,23 +537,26 @@
             entity_tiles(2, "curve")
 
     together([entity_stream(h) for h in range(NS)])
-    for e in range(NB):
-        emsg[0, e // 2, pl.ds(e % 2, 1), :] = curve_row(plan[E_LAST, e])
-    small = []
-    for d in range(1, 8):
-        there = lax.rem(row + d, 8)
-        small.append(copies.start(emsg.at[0, there], emsg.at[1, row], (there, col)))
-    emsg[1, row] = emsg[0, row]
+    for n, d in enumerate(FAR + (0,)):
+        y = lax.rem(cy + d, 4)
+        for c in range(2):
+            for m in range(2):
+                emsg[c, n, m : m + 1] = curve_row(plan[E_LAST, (y * 2 + c) * 2 + m])
+    first = copies.start(emsg.at[1 - cc], ecome, mate)
     mine = jnp.sum(
-        jnp.where(lax.broadcasted_iota(jnp.int32, (NB, B), 0) == col, total, 0.0),
+        jnp.where(lax.broadcasted_iota(jnp.int32, (NB, B), 0) == col, rates, 0.0),
         axis=0, keepdims=True,
     )
-    step = to_column(cmsg[col, pl.ds(NB, 1), :] / (mine + eps))
-    x_out[...] = (vx[...] + step * vd[...]).astype(BF16)
+    x_out[...] = (vx[...] + to_column(mine) * vd[...]).astype(BF16)
+    arrived([first])
+    small = []
+    for n, d in enumerate(FAR):
+        esum[n] = emsg[cc, n] + ecome[n]
+        small.append(copies.start(esum.at[n], elast.at[n], at_y(d)))
+    total = emsg[cc, 3] + ecome[3]
     arrived(small)
-    total = emsg[1, 0]
-    for n in range(1, 8):
-        total = total + emsg[1, n]
+    for n in range(3):
+        total = total + elast[n]
     for m in range(2):
         rows = pl.ds(m * B, B)
         step = un[rows, :][:, :1] / (to_column(total[m : m + 1]) + uq[rows, :][:, :1] + eps)
@@ -574,11 +570,6 @@
 
 
 def on_device(alias_factors, entity_factors, tile_ids, tile_score, tile_weight):
-    plan = pl.pallas_call(
-        plan_kernel,
-        name="tile_plan",
-        out_shape=jax.ShapeDtypeStruct((16, 128), jnp.int32),
-    )(tile_ids[0, 0].T)
     vmem = pl.BlockSpec(memory_space=pltpu.VMEM)
     hbm = pl.BlockSpec(memory_space=pl.ANY)
     V = pltpu.VMEM
@@ -593,7 +584,7 @@
             jax.ShapeDtypeStruct((B, K), BF16),
             jax.ShapeDtypeStruct((2 * B, K), BF16),
         ),
-        in_specs=[pl.BlockSpec(memory_space=pltpu.SMEM), vmem, vmem, hbm, hbm],
+        in_specs=[vmem, vmem, vmem, hbm, hbm],
         out_specs=(vmem, vmem),
         scratch_shapes=[
             V((T + 1, B, B), BF16), V((T + 1, B, B), BF16),
@@ -604,22 +595,24 @@
             V((NB, B, K), BF16), each(2, (NB, R, K), BF16),
             each(2, (4, 4, R, B), BF16), each(2, (4, 4, R, B), BF16),
             each(2, (3, 4, R, B), BF16), each(2, (3, 4, R, B), BF16),
-            each(2, (3, R, B), BF16), each(2, (3, R, B), BF16),
-            each(2, (3, R, B), BF16), each(2, (3, R, B), BF16),
+            each(2, (3, R, B), F32), each(2, (3, R, B), F32),
+            each(2, (3, R, B), F32), each(2, (3, R, B), F32),
             each(2, (2, 4, 2, R, K), F32), each(2, (4, 2, R, K), F32),
             each(2, (3, 2, R, K), BF16), each(2, (3, 2, R, K), BF16),
-            V((NB, NB + 8, B), F32), V((2, 8, 8, B), F32),
+            V((4, 2 * NB, B), F32), V((4, 2 * NB, B), F32),
+            V((2, 4, 8, B), F32), V((4, 8, B), F32), V((3, 8, B), F32), V((3, 8, B), F32),
             V((B, K), F32), V((B, K), F32), V((B, K), F32), V((B, B), F32), V((B, B), F32),
             V((2 * B, K), F32), V((2 * B, K), F32), V((2 * B, K), F32),
             V((2 * B, B), F32), V((2 * B, B), F32),
+            V((16, 128), jnp.int32), pltpu.SMEM((16, 128), jnp.int32),
             pltpu.SemaphoreType.DMA((N_COPIES,)),
             pltpu.SemaphoreType.DMA((N_COPIES,)),
-            pltpu.SemaphoreType.DMA((2,)),
+            pltpu.SemaphoreType.DMA((3,)),
         ],
         compiler_params=pltpu.CompilerParams(
             collective_id=0, has_side_effects=True, vmem_limit_bytes=60 * 2**20
         ),
-    )(plan, alias_factors, entity_factors, tile_weight, tile_score)
+    )(tile_ids[0, 0].T, alias_factors, entity_factors, tile_weight, tile_score)
     return pl.pallas_call(
         emit_kernel,
         name="emit",

time: 137 us -> 138 us (level)
  Pallas kernels: 135 us -> 137 us
    pallas_call x1, Pallas kernels: 132 us -> 135 us  [on_device(): pl.pallas_call(sweep_kernel, name='als_sweep', out_shape=(jax.ShapeDtypeS...]
    pallas_call x1 -> x0, Pallas kernels: 1.63 us -> none  [on_device(): pl.pallas_call(plan_kernel, name='tile_plan', out_shape=jax.ShapeDtypeStr...]
where the time goes in v3:
time: 138 us
  Pallas kernels  137 us (99%)
    pallas_call x1, Pallas kernels, on_device(): pl.pallas_call(sweep_kernel, name='als_sweep', out_shape=(jax.ShapeDtypeS...  135 us

profile of v3, /device:TPU:0, one launch (start us, length us, event | category | flops | bytes accessed | tf_op | source)
XLA Modules:
  0.0 137.6 jit_solution(10928492546716713774)
XLA Ops:
  0.6 135.4 %als_sweep.1 = (bf16[128,256]{1,0:T(8,128)(2,1)}, bf16[256,256]{1,0:T(8,128)(2,1)}) custom-call(s32[2,96]{1,0:T(2,128)} %bitcast.3, bf16[128,256]{1,0:T(8,128)(2,1)} %x_in.1, bf16[256,256]{1,0:T(8,128)(2,1)} %y_in.1, bf16[1,1,96,128,128]{4,3,2,1,0:T(8,128)(2,1)} %w_hbm.1, bf16[1,1,96,128,128]{4,3,2,1,0:T(8,128)(2,1)} %s_hbm.1), custom_call_target="tpu_custom_call" | custom-call | tf_op jit(solution)/shard_map/als_sweep/pallas_call | solution.py:580
  136.0 1.6 %emit.1 = (bf16[128,256]{1,0:T(8,128)(2,1)}, bf16[256,256]{1,0:T(8,128)(2,1)}) custom-call(bf16[128,256]{1,0:T(8,128)(2,1)} %get-tuple-element.4.x_in, bf16[256,256]{1,0:T(8,128)(2,1)} %get-tuple-element.5.y_in), custom_call_target="tpu_custom_call" | custom-call | tf_op jit(solution)/shard_map/emit/pallas_call | solution.py:616

commit v4 on v3

--- a/solution.py
+++ b/solution.py
@@ -110,10 +110,10 @@
 
 
 def sweep_kernel(
-    ids, x_in, y_in, w_hbm, s_hbm, x_out, y_out,
+    ids, x_hbm, y_hbm, w_hbm, s_hbm, x_out, y_out,
     w, s, wt, st, xn, run, run_c, ga, gb, gy0, gy, sa, sb, ra, rb, ta, tb, qa, qb,
     se, me, te, qe, cmsg, csum, emsg, ecome, esum, elast, vx, vr, vd, vn, vq, ux, ur, ud, un, uq,
-    plan_v, plan, send, recv, lsem,
+    x_in, y_in, plan_v, plan, send, recv, lsem,
 ):
     row = lax.axis_index("row")
     col = lax.axis_index("col")
@@ -135,8 +135,10 @@
     load_w = pltpu.make_async_copy(w_hbm.at[0, 0], w.at[pl.ds(0, T)], lsem.at[0])
     load_s = pltpu.make_async_copy(s_hbm.at[0, 0], s.at[pl.ds(0, T)], lsem.at[1])
     load_plan = pltpu.make_async_copy(plan_v, plan, lsem.at[2])
-    load_w.start()
-    load_s.start()
+    load_x = pltpu.make_async_copy(x_hbm, x_in, lsem.at[3])
+    load_y = pltpu.make_async_copy(y_hbm, y_in, lsem.at[4])
+    load_x.start()
+    load_y.start()
 
     barrier = pltpu.get_barrier_semaphore()
     for peer in [at(d) for at in (at_x, at_z, at_y) for d in FAR] + [mate]:
@@ -157,6 +159,9 @@
     def arrived(list_of_copies):
         for cp in list_of_copies:
             cp.wait_recv()
+
+    load_x.wait()
+    load_y.wait()
 
     def alias_gather(i, h, value):
         a, b = ga[i][h], gb[i][h]
@@ -396,28 +401,30 @@
         x0 = x_in[rows, :]
         mid = alias_gather(0, h, x0)
         if h == 0:
-            mid_y = entity_gather(gy0, [y_in[pl.ds(0, B), :], y_in[pl.ds(B, B), :]])
+            own_y = [y_in[pl.ds(0, B), :], y_in[pl.ds(B, B), :]]
+            y_gather.append(entity_gather(gy0, own_y))
+            load_w.start()
+            load_s.start()
         yield
         second = mid()
-        if h == 0:
+        if h == NS - 1:
             tile_plan(ids, plan_v, cx, cz)
             load_plan.start()
-            y_gather.append(mid_y())
+            run[0] = jnp.zeros((B, K), F32)
+            run_c[0] = jnp.zeros((B, B), F32)
+            emsg[...] = jnp.zeros_like(emsg)
             load_plan.wait()
             load_w.wait()
             load_s.wait()
             zero = jnp.zeros((B, B), BF16)
             for ref in (w, s, wt, st):
                 ref[T] = zero
-            run[0] = jnp.zeros((B, K), F32)
-            run_c[0] = jnp.zeros((B, B), F32)
-            emsg[...] = jnp.zeros_like(emsg)
-        if h == NS - 1:
+            y_gather.append(y_gather[0]())
             gap()
         yield
         arrived(second)
         if h == NS - 1:
-            arrived(y_gather[0])
+            arrived(y_gather[1])
             alias_tiles(0, "resid")
         yield
         middle, end = alias_spread(0, h)
@@ -554,6 +561,7 @@
         esum[n] = emsg[cc, n] + ecome[n]
         small.append(copies.start(esum.at[n], elast.at[n], at_y(d)))
     total = emsg[cc, 3] + ecome[3]
+    copies.flush(copies.all[:-3])
     arrived(small)
     for n in range(3):
         total = total + elast[n]
@@ -584,7 +592,7 @@
             jax.ShapeDtypeStruct((B, K), BF16),
             jax.ShapeDtypeStruct((2 * B, K), BF16),
         ),
-        in_specs=[vmem, vmem, vmem, hbm, hbm],
+        in_specs=[vmem, hbm, hbm, hbm, hbm],
         out_specs=(vmem, vmem),
         scratch_shapes=[
             V((T + 1, B, B), BF16), V((T + 1, B, B), BF16),
@@ -604,10 +612,11 @@
             V((B, K), F32), V((B, K), F32), V((B, K), F32), V((B, B), F32), V((B, B), F32),
             V((2 * B, K), F32), V((2 * B, K), F32), V((2 * B, K), F32),
             V((2 * B, B), F32), V((2 * B, B), F32),
+            V((B, K), BF16), V((2 * B, K), BF16),
             V((16, 128), jnp.int32), pltpu.SMEM((16, 128), jnp.int32),
             pltpu.SemaphoreType.DMA((N_COPIES,)),
             pltpu.SemaphoreType.DMA((N_COPIES,)),
-            pltpu.SemaphoreType.DMA((3,)),
+            pltpu.SemaphoreType.DMA((5,)),
         ],
         compiler_params=pltpu.CompilerParams(
             collective_id=0, has_side_effects=True, vmem_limit_bytes=60 * 2**20

time: 138 us -> 136 us (0.986)
  Pallas kernels: 137 us -> 135 us
    pallas_call x1, Pallas kernels: 135 us -> 134 us  [on_device(): pl.pallas_call(sweep_kernel, name='als_sweep', out_shape=(jax.ShapeDtypeS...]
where the time goes in v4:
time: 136 us
  Pallas kernels  135 us (99%)
    pallas_call x1, Pallas kernels, on_device(): pl.pallas_call(sweep_kernel, name='als_sweep', out_shape=(jax.ShapeDtypeS...  134 us

profile of v4, /device:TPU:0, one launch (start us, length us, event | category | flops | bytes accessed | tf_op | source)
XLA Modules:
  0.0 136.1 jit_solution(1802172560296705284)
XLA Ops:
  0.6 133.8 %als_sweep.1 = (bf16[128,256]{1,0:T(8,128)(2,1)}, bf16[256,256]{1,0:T(8,128)(2,1)}) custom-call(s32[2,96]{1,0:T(2,128)} %bitcast.3, bf16[128,256]{1,0:T(8,128)(2,1)} %x_hbm.1, bf16[256,256]{1,0:T(8,128)(2,1)} %y_hbm.1, bf16[1,1,96,128,128]{4,3,2,1,0:T(8,128)(2,1)} %w_hbm.1, bf16[1,1,96,128,128]{4,3,2,1,0:T(8,128)(2,1)} %s_hbm.1), custom_call_target="tpu_custom_call" | custom-call | tf_op jit(solution)/shard_map/als_sweep/pallas_call | solution.py:588
  134.4 1.6 %emit.1 = (bf16[128,256]{1,0:T(8,128)(2,1)}, bf16[256,256]{1,0:T(8,128)(2,1)}) custom-call(bf16[128,256]{1,0:T(8,128)(2,1)} %get-tuple-element.4.x_in, bf16[256,256]{1,0:T(8,128)(2,1)} %get-tuple-element.5.y_in), custom_call_target="tpu_custom_call" | custom-call | tf_op jit(solution)/shard_map/emit/pallas_call | solution.py:625

commit v5 on v4

--- a/solution.py
+++ b/solution.py
@@ -462,13 +462,12 @@
         vq[rows, :] = jnp.broadcast_to(ridge * jnp.sum(d1 * d1, axis=-1, keepdims=True), (R, B))
         yield
         second = mid()
+        mid_x = alias_gather(3, h, vx[rows, :].astype(BF16))
         if h == NS - 1:
             gap()
         yield
-        mid_x = alias_gather(3, h, vx[rows, :].astype(BF16))
+        x_gather.extend(mid_x())
         arrived(second)
-        yield
-        x_gather.extend(mid_x())
         if h == NS - 1:
             alias_tiles(2, "curve")
 

time: 136 us -> 135 us (level)
    pallas_call x1, Pallas kernels: 134 us -> 132 us  [on_device(): pl.pallas_call(sweep_kernel, name='als_sweep', out_shape=(jax.ShapeDtypeS...]
where the time goes in v5:
time: 135 us
  Pallas kernels  134 us (99%)
    pallas_call x1, Pallas kernels, on_device(): pl.pallas_call(sweep_kernel, name='als_sweep', out_shape=(jax.ShapeDtypeS...  132 us

profile of v5, /device:TPU:0, one launch (start us, length us, event | category | flops | bytes accessed | tf_op | source)
XLA Modules:
  0.0 134.6 jit_solution(13283067512434196962)
XLA Ops:
  0.6 132.3 %als_sweep.1 = (bf16[128,256]{1,0:T(8,128)(2,1)}, bf16[256,256]{1,0:T(8,128)(2,1)}) custom-call(s32[2,96]{1,0:T(2,128)} %bitcast.3, bf16[128,256]{1,0:T(8,128)(2,1)} %x_hbm.1, bf16[256,256]{1,0:T(8,128)(2,1)} %y_hbm.1, bf16[1,1,96,128,128]{4,3,2,1,0:T(8,128)(2,1)} %w_hbm.1, bf16[1,1,96,128,128]{4,3,2,1,0:T(8,128)(2,1)} %s_hbm.1), custom_call_target="tpu_custom_call" | custom-call | tf_op jit(solution)/shard_map/als_sweep/pallas_call | solution.py:587
  133.0 1.6 %emit.1 = (bf16[128,256]{1,0:T(8,128)(2,1)}, bf16[256,256]{1,0:T(8,128)(2,1)}) custom-call(bf16[128,256]{1,0:T(8,128)(2,1)} %get-tuple-element.4.x_in, bf16[256,256]{1,0:T(8,128)(2,1)} %get-tuple-element.5.y_in), custom_call_target="tpu_custom_call" | custom-call | tf_op jit(solution)/shard_map/emit/pallas_call | solution.py:624
